TPU v7x, 512 devices: a whole 4x4x16 slice. The times are simulated.
512 devices in a mesh: rep: 32 (over x_lo, z), fsdp: 16 (over y, x_hi, core).
Axes of the slice: x: 4 (x_hi: 2, x_lo: 2; x = x_hi * 2 + x_lo), y: 4, z: 16, core: 2. Of those that a mesh axis runs over, the one named last changes fastest.
Arguments:
- master: float32 [32, 8192, 512], P('rep', 'fsdp'), may hold values from -6 to 6
- features: bfloat16 [32, 2048, 8192], P('rep', 'fsdp'), may hold values from -6 to 6
- targets: bfloat16 [32, 2048, 512], P('rep', 'fsdp'), may hold values from -6 to 6
Outputs:
- updated: float32 [32, 8192, 512], P('rep', 'fsdp')
All inputs are finite; a program needn't handle non-finite values.
Results may differ from a plain program's by a relative error of at most 0.0024.
Values may be sent and summed in bfloat16 or wider, within the bound.
No kernel may reach another device: no remote copies, remote signals or barrier semaphores. Data moves between devices by JAX's collectives and lax.ppermute only.
A program may use at most 64 MiB of HBM per device.

v0:
```python
import jax
import jax.numpy as jnp
from jax import lax
from jax.sharding import PartitionSpec as P

D = 8192
STEP = 3


def from_behind(block, axis, distance):
    devices = range(lax.axis_size(axis))
    route = [((i - distance) % len(devices), i) for i in devices]
    return lax.ppermute(block, axis, route)


def body(master, features, targets):
    scale = 1.0 / D**0.5
    levels = lax.axis_size("rep").bit_length() - 1
    hop = 2 ** (STEP % levels)
    own_master = master[0]
    tokens = features[0]
    working = own_master.astype(jnp.bfloat16)
    columns = lax.all_to_all(tokens, "fsdp", split_axis=1, concat_axis=0, tiled=True)
    summed = jnp.dot(
        tokens,
        lax.all_gather(working, "fsdp", axis=0, tiled=True),
        preferred_element_type=jnp.float32,
    )
    error = (summed * scale - targets[0].astype(jnp.float32)).astype(jnp.bfloat16)
    grad = (
        lax.dot_general(
            columns,
            lax.all_gather(error, "fsdp", axis=0, tiled=True),
            (((0,), (0,)), ((), ())),
            preferred_element_type=jnp.float32,
        )
        * scale
    )
    stepped = own_master - 0.5 * grad
    other = from_behind(stepped, "rep", hop)
    updated = 0.5 * (stepped + other)
    return updated[None]


def solution(mesh):
    return jax.shard_map(
        body,
        mesh=mesh,
        in_specs=(P("rep", "fsdp", None), P("rep", "fsdp", None), P("rep", "fsdp", None)),
        out_specs=P("rep", "fsdp", None),
        check_vma=False,
    )
```

profile of v0, /device:TPU:8, one launch (start us, length us, event | category | flops | bytes accessed | tf_op | source)
XLA Modules:
  0.0 293.4 jit_solution(9856002169636224841)
XLA Ops:
  6.5 0.0 copy-start
  6.5 0.0 copy-start.1
  6.5 0.0 all-gather.3.cloned.1.call-start
  6.5 1.7 copy.8
  8.3 0.9 bitcast_convert_fusion
  9.1 0.0 all-gather.3.cloned.1.call-update
  9.1 0.0 all-gather.5.cloned.1.call-start
  9.2 96.7 %all-gather.3.cloned.1.call-done = bf16[8192,512]{0,1:T(8,128)(2,1)} async-done(((bf16[512,512]{0,1:T(8,128)(2,1)}), bf16[8192,512]{0,1:T(8,128)(2,1)}) %all-gather.3.cloned.1.call-update) | async-done | bytes 8388624 | tf_op jit(solution)/shard_map/all_gather | solution.py:26
  105.8 0.0 copy-done
  105.9 0.0 copy-done.1
  105.9 7.0 %fusion.10 = bf16[128,512]{1,0:T(8,128)(2,1)} fusion(bf16[8192,512]{0,1:T(8,128)(2,1)} %all-gather.3.cloned.1.call-done, bf16[1,128,8192]{2,1,0:T(8,128)(2,1)S(1)} %copy-done, bf16[1,128,512]{2,1,0:T(8,128)(2,1)S(1)} %copy-done.1), kind=kOutput, calls=%fused_computation.7 | convolution fusion | flops 1074003968 | bytes 10747904 | tf_op jit(solution)/shard_map/dot_general | solution.py:24
  112.8 0.0 all-gather.5.cloned.1.call-update
  112.8 3.2 %copy.9 = bf16[1,128,8192]{1,2,0:T(8,128)(2,1)S(1)} copy(bf16[1,128,8192]{2,1,0:T(8,128)(2,1)} %param.4) | data formatting | bytes 4194304 | tf_op args[1]
  116.1 33.3 %all_to_all.19 = bf16[128,16,512]{0,2,1:T(8,128)(2,1)} all-to-all(bf16[128,16,512]{0,2,1:T(8,128)(2,1)S(1)} %bitcast.29), channel_id=1, replica_groups=mesh['rep'=32,'fsdp'=16] {'fsdp'}, dimensions={1} | all-to-all | bytes 4194304 | tf_op jit(solution)/shard_map/all_to_all | solution.py:23
  149.4 2.9 copy.10
  152.2 26.9 %all-gather.5.cloned.1.call-done = bf16[2048,512]{1,0:T(8,128)(2,1)} async-done(((bf16[128,512]{1,0:T(8,128)(2,1)}), bf16[2048,512]{1,0:T(8,128)(2,1)}) %all-gather.5.cloned.1.call-update) | async-done | bytes 2097168 | tf_op jit(solution)/shard_map/all_gather | solution.py:33
  179.2 2.9 fusion.3
  182.1 12.8 %collective-permute-start = (f32[512,512]{0,1:T(8,128)S(1)}, f32[512,512]{0,1:T(8,128)S(1)}, u32[]{:S(2)}, u32[]{:S(2)}) collective-permute-start(f32[512,512]{0,1:T(8,128)S(1)} %fusion.3), channel_id=1, source_target_pairs={{384,0},{400,16},{416,32},{432,48},{448,64},{464,80},{480,96},{496... | collective-permute-start | bytes 3145736 | tf_op jit(solution)/shard_map/ppermute | solution.py:13
  194.9 90.1 %collective-permute-done = f32[512,512]{0,1:T(8,128)S(1)} collective-permute-done((f32[512,512]{0,1:T(8,128)S(1)}, f32[512,512]{0,1:T(8,128)S(1)}, u32[]{:S(2)}, u32[]{:S(2)}) %collective-permute-start) | collective-permute-done | bytes 1048608 | tf_op jit(solution)/shard_map/ppermute | solution.py:13
  285.0 0.2 multiply_bitcast_fusion
  285.2 1.3 copy.11
Async XLA Ops:
  6.5 99.3 %copy-start = (bf16[1,128,8192]{2,1,0:T(8,128)(2,1)S(1)}, bf16[1,128,8192]{2,1,0:T(8,128)(2,1)}, u32[]{:S(2)}) copy-start(bf16[1,128,8192]{2,1,0:T(8,128)(2,1)} %param.4) | copy-start | bytes 6291460
  6.5 99.3 %copy-start.1 = (bf16[1,128,512]{2,1,0:T(8,128)(2,1)S(1)}, bf16[1,128,512]{2,1,0:T(8,128)(2,1)}, u32[]{:S(2)}) copy-start(bf16[1,128,512]{2,1,0:T(8,128)(2,1)} %param.5) | copy-start | bytes 393220
  6.5 99.3 %all-gather.3.cloned.1.call-start = ((), (), s32[]{:S(2)}) async-start(), calls=%async_computation.1 | async-start | bytes 8912896 | tf_op jit(solution)/shard_map/all_gather | solution.py:26
  9.1 170.0 %all-gather.5.cloned.1.call-start = ((), (), s32[]{:S(2)}) async-start(), calls=%async_computation.2 | async-start | bytes 2228224 | tf_op jit(solution)/shard_map/all_gather | solution.py:33
  182.1 102.9 %collective-permute-start = (f32[512,512]{0,1:T(8,128)S(1)}, f32[512,512]{0,1:T(8,128)S(1)}, u32[]{:S(2)}, u32[]{:S(2)}) collective-permute-start(f32[512,512]{0,1:T(8,128)S(1)} %fusion.3), channel_id=1, source_target_pairs={{384,0},{400,16},{416,32},{432,48},{448,64},{464,80},{480,96},{496... | collective-permute-start | bytes 3145736 | tf_op jit(solution)/shard_map/ppermute | solution.py:13
Sparse Core Ops, SparseCore 0:
  10.6 95.2 all-gather.2
  113.0 66.1 all-gather.4
where the time goes:
time: 294 us; the launch traced here: 293 us
  waiting for transfers between devices  214 us (73%)
  blocking collectives  33.3 us (11%)
  between operations  13.4 us (5%)
  starting transfers between devices  12.9 us (4%)
  matrix products  9.83 us (3%)
  local copies, waits for them, and re-layouts  9.1 us (3%)
    all_gather x1, waiting for transfers between devices, body(): lax.all_gather(working, 'fsdp', axis=0, tiled=True)  96.7 us
    ppermute x1, waiting for transfers between devices, from_behind(): return lax.ppermute(block, axis, route)  90.1 us
    all_to_all x1, blocking collectives, body(): lax.all_to_all(tokens, 'fsdp', split_axis=1, concat_axis=0, tiled=True)  33.3 us
    all_gather x1, waiting for transfers between devices, body(): lax.all_gather(error, 'fsdp', axis=0, tiled=True)  26.9 us
    ppermute x1, starting transfers between devices, from_behind(): return lax.ppermute(block, axis, route)  12.8 us
    dot_general x1, matrix products, body(): jnp.dot(tokens, lax.all_gather(working, 'fsdp', axis=0, tiled=True), pref...  6.96 us
  transfers between devices with their start and end apart: 3, of which 3 were waited for; matrix products, arithmetic and copies ran while one was open for 2% of the time, Pallas kernels for 0%

commit v1 on v0

v1 whole, which is shorter than its diff:
```python
import jax
import jax.numpy as jnp
from jax import lax
from jax.sharding import PartitionSpec as P

D = 8192
STEP = 3
CHUNKS = 4


def from_behind(block, axis, distance):
    devices = range(lax.axis_size(axis))
    route = [((i - distance) % len(devices), i) for i in devices]
    return lax.ppermute(block, axis, route)


def body(master, features, targets):
    scale = 1.0 / D**0.5
    levels = lax.axis_size("rep").bit_length() - 1
    hop = 2 ** (STEP % levels)
    size = lax.axis_size("fsdp")
    chips = size // 2
    core = lax.axis_index("fsdp") % 2
    groups = [list(range(c, size, 2)) for c in range(2)]
    swap_route = [(i, i ^ 1) for i in range(size)]

    def exchange(blocks):
        return lax.all_to_all(blocks, "fsdp", 0, 0, axis_index_groups=groups)

    def swap(block):
        return lax.ppermute(block, "fsdp", swap_route)

    own_master = master[0]
    rows, width = own_master.shape
    tokens = features[0]
    count = tokens.shape[0]
    depth = 2 * rows

    working = own_master.astype(jnp.bfloat16)
    peer = swap(working)
    first = jnp.where(core == 0, working, peer)
    second = jnp.where(core == 0, peer, working)
    weights = jnp.concatenate([first, second], axis=0)

    columns = exchange(tokens.reshape(count, chips, depth).transpose(1, 0, 2))
    columns = columns.reshape(chips * count, depth)

    step = width // CHUNKS
    results = []
    for c in range(CHUNKS):
        part = slice(c * step, (c + 1) * step)
        partial = jnp.dot(columns, weights[:, part], preferred_element_type=jnp.float32)
        partial = (partial * scale).astype(jnp.bfloat16).reshape(chips, count, step)
        keys = exchange(partial).astype(jnp.float32).sum(axis=0)
        error = (keys - targets[0][:, part].astype(jnp.float32)).astype(jnp.bfloat16)
        errors = exchange(jnp.broadcast_to(error, (chips, count, step)))
        grad = lax.dot_general(
            columns,
            errors.reshape(chips * count, step),
            (((0,), (0,)), ((), ())),
            preferred_element_type=jnp.float32,
        ).reshape(2, rows, step)
        kept = lax.dynamic_index_in_dim(grad, core, 0, keepdims=False)
        given = lax.dynamic_index_in_dim(grad, 1 - core, 0, keepdims=False)
        grad = kept + swap(given)
        stepped = own_master[:, part] - (0.5 * scale) * grad
        other = from_behind(stepped.astype(jnp.bfloat16), "rep", hop)
        results.append(0.5 * (stepped + other.astype(jnp.float32)))
    return jnp.concatenate(results, axis=1)[None]


def solution(mesh):
    return jax.shard_map(
        body,
        mesh=mesh,
        in_specs=(P("rep", "fsdp", None), P("rep", "fsdp", None), P("rep", "fsdp", None)),
        out_specs=P("rep", "fsdp", None),
        check_vma=False,
    )
```

time: 294 us -> 244 us (0.83)
  the two profiles are of different devices: /device:TPU:8 before, /device:TPU:1 now
where the time goes in v1:
time: 244 us; the launch traced here: 242 us
  starting transfers between devices  91.6 us (38%)
  waiting for transfers between devices  79.4 us (33%)
  local copies, waits for them, and re-layouts  33.5 us (14%)
  matrix products  16 us (7%)
  blocking collectives  10.7 us (4%)
  other arithmetic  9.94 us (4%)
    all_to_all x8, waiting for transfers between devices, exchange(): return lax.all_to_all(blocks, 'fsdp', 0, 0, axis_index_groups=groups)  41.2 us
    all_to_all x8, starting transfers between devices, exchange(): return lax.all_to_all(blocks, 'fsdp', 0, 0, axis_index_groups=groups)  38.1 us
    ppermute x4, waiting for transfers between devices, from_behind(): return lax.ppermute(block, axis, route)  36.1 us
    ppermute x4, starting transfers between devices, from_behind(): return lax.ppermute(block, axis, route)  31.4 us
    ppermute x5, starting transfers between devices, swap(): return lax.ppermute(block, 'fsdp', swap_route)  22.1 us
    all_to_all x1, blocking collectives, exchange(): return lax.all_to_all(blocks, 'fsdp', 0, 0, axis_index_groups=groups)  10.7 us
    dot_general x4, matrix products, body(): lax.dot_general(columns, errors.reshape(chips * count, step), (((0,), (0,...  8.77 us
    reshape x4, local copies, waits for them, and re-layouts, body(): grad = lax.dot_general(columns, errors.reshape(chips * count, step), (((0...  8.36 us
  transfers between devices with their start and end apart: 17, of which 11 were waited for; matrix products, arithmetic and copies ran while one was open for 19% of the time, Pallas kernels for 0%

profile of v1, /device:TPU:1, one launch (start us, length us, event | category | flops | bytes accessed | tf_op | source)
XLA Modules:
  0.0 241.5 jit_solution(16431039810057196130)
XLA Ops:
  0.0 3.2 %copy.30 = bf16[1,128,8192]{1,2,0:T(8,128)(2,1)S(1)} copy(bf16[1,128,8192]{2,1,0:T(8,128)(2,1)} %param.4) | data formatting | bytes 4194304 | tf_op args[1]
  3.2 2.6 %copy.31 = bf16[128,8,1024]{2,0,1:T(8,128)(2,1)} copy(bf16[128,8,1024]{0,2,1:T(8,128)(2,1)S(1)} %bitcast.121) | data formatting | bytes 4194304 | tf_op jit(solution)/shard_map/reshape;squeeze | solution.py:45
  5.8 7.6 %all-to-all-start = ((bf16[8,128,1024]{2,1,0:T(8,128)(2,1)}), bf16[8,128,1024]{2,1,0:T(8,128)(2,1)S(1)}, u32[]{:S(2)}, u32[]{:S(2)}) async-start(bf16[8,128,1024]{2,1,0:T(8,128)(2,1)} %bitcast.120), calls=%async_computation | async-start | bytes 4194304 | tf_op jit(solution)/shard_map/all_to_all | solution.py:28
  14.3 4.9 %collective-permute-start = (bf16[512,512]{1,0:T(8,128)(2,1)}, bf16[512,512]{1,0:T(8,128)(2,1)}, u32[]{:S(2)}, u32[]{:S(2)}) collective-permute-start(bf16[512,512]{1,0:T(8,128)(2,1)} %bitcast_convert_fusion), channel_id=1, source_target_pairs={{0,1},{1,0},{2,3},{3,2},{4,5},{5,4},{6,7},{7,6},{8,9},{9,8},{10,11... | collective-permute-start | bytes 1572872 | tf_op jit(solution)/shard_map/ppermute | solution.py:31
  23.2 15.5 %all-to-all-done = bf16[8,128,1024]{2,1,0:T(8,128)(2,1)S(1)} async-done(((bf16[8,128,1024]{2,1,0:T(8,128)(2,1)}), bf16[8,128,1024]{2,1,0:T(8,128)(2,1)S(1)}, u32[]{:S(2)}, u32[]{:S(2)}) %all-to-all-start) | async-done | bytes 2097184 | tf_op jit(solution)/shard_map/all_to_all | solution.py:28
  41.2 5.6 %all-to-all-start.1 = ((bf16[8,128,128]{1,2,0:T(8,128)(2,1)}), bf16[8,128,128]{1,2,0:T(8,128)(2,1)S(1)}, u32[]{:S(2)}, u32[]{:S(2)}) async-start(bf16[8,128,128]{1,2,0:T(8,128)(2,1)} %bitcast.125), calls=%async_computation.1 | async-start | bytes 524288 | tf_op jit(solution)/shard_map/all_to_all | solution.py:28
  50.4 4.3 %all-to-all-done.1 = bf16[8,128,128]{1,2,0:T(8,128)(2,1)S(1)} async-done(((bf16[8,128,128]{1,2,0:T(8,128)(2,1)}), bf16[8,128,128]{1,2,0:T(8,128)(2,1)S(1)}, u32[]{:S(2)}, u32[]{:S(2)}) %all-to-all-start.1) | async-done | bytes 262176 | tf_op jit(solution)/shard_map/all_to_all | solution.py:28
  54.7 4.1 %all-to-all-start.7 = ((bf16[8,128,128]{1,2,0:T(8,128)(2,1)}), bf16[8,128,128]{1,2,0:T(8,128)(2,1)}, u32[]{:S(2)}, u32[]{:S(2)}) async-start(bf16[8,128,128]{1,2,0:T(8,128)(2,1)} %bitcast.124), calls=%async_computation.7 | async-start | bytes 524288 | tf_op jit(solution)/shard_map/all_to_all | solution.py:28
  61.3 5.1 %all-to-all-done.7 = bf16[8,128,128]{1,2,0:T(8,128)(2,1)} async-done(((bf16[8,128,128]{1,2,0:T(8,128)(2,1)}), bf16[8,128,128]{1,2,0:T(8,128)(2,1)}, u32[]{:S(2)}, u32[]{:S(2)}) %all-to-all-start.7) | async-done | bytes 262176 | tf_op jit(solution)/shard_map/all_to_all | solution.py:28
  66.5 4.0 %all-to-all-start.5 = ((bf16[8,128,128]{1,2,0:T(8,128)(2,1)}), bf16[8,128,128]{1,2,0:T(8,128)(2,1)}, u32[]{:S(2)}, u32[]{:S(2)}) async-start(bf16[8,128,128]{1,2,0:T(8,128)(2,1)} %bitcast.122), calls=%async_computation.5 | async-start | bytes 524288 | tf_op jit(solution)/shard_map/all_to_all | solution.py:28
  73.8 4.4 %all-to-all-done.5 = bf16[8,128,128]{1,2,0:T(8,128)(2,1)} async-done(((bf16[8,128,128]{1,2,0:T(8,128)(2,1)}), bf16[8,128,128]{1,2,0:T(8,128)(2,1)}, u32[]{:S(2)}, u32[]{:S(2)}) %all-to-all-start.5) | async-done | bytes 262176 | tf_op jit(solution)/shard_map/all_to_all | solution.py:28
  78.2 3.4 %all-to-all-start.3 = ((bf16[8,128,128]{1,2,0:T(8,128)(2,1)}), bf16[8,128,128]{1,2,0:T(8,128)(2,1)S(1)}, u32[]{:S(2)}, u32[]{:S(2)}) async-start(bf16[8,128,128]{1,2,0:T(8,128)(2,1)} %bitcast.123), calls=%async_computation.3 | async-start | bytes 524288 | tf_op jit(solution)/shard_map/all_to_all | solution.py:28
  84.8 4.3 %all-to-all-done.3 = bf16[8,128,128]{1,2,0:T(8,128)(2,1)S(1)} async-done(((bf16[8,128,128]{1,2,0:T(8,128)(2,1)}), bf16[8,128,128]{1,2,0:T(8,128)(2,1)S(1)}, u32[]{:S(2)}, u32[]{:S(2)}) %all-to-all-start.3) | async-done | bytes 262176 | tf_op jit(solution)/shard_map/all_to_all | solution.py:28
  90.8 10.7 %all_to_all.45 = bf16[8,128,128]{1,2,0:T(8,128)(2,1)} all-to-all(bf16[8,128,128]{1,2,0:T(8,128)(2,1)S(1)} %broadcast_in_dim.16), channel_id=1, replica_groups={{0,2,4,6,8,10,12,14},{1,3,5,7,9,11,13,15},{16,18,20,22,24,26,28,30},{17..., dimensions={0} | all-to-all | bytes 524288 | tf_op jit(solution)/shard_map/all_to_all | solution.py:28
  102.3 3.4 %all-to-all-start.2 = ((bf16[8,128,128]{1,2,0:T(8,128)(2,1)}), bf16[8,128,128]{1,2,0:T(8,128)(2,1)S(1)}, u32[]{:S(2)}, u32[]{:S(2)}) async-start(bf16[8,128,128]{1,2,0:T(8,128)(2,1)} %broadcast_in_dim.15), calls=%async_computation.2 | async-start | bytes 524288 | tf_op jit(solution)/shard_map/all_to_all | solution.py:28
  105.7 7.6 %all-to-all-done.2 = bf16[8,128,128]{1,2,0:T(8,128)(2,1)S(1)} async-done(((bf16[8,128,128]{1,2,0:T(8,128)(2,1)}), bf16[8,128,128]{1,2,0:T(8,128)(2,1)S(1)}, u32[]{:S(2)}, u32[]{:S(2)}) %all-to-all-start.2) | async-done | bytes 262176 | tf_op jit(solution)/shard_map/all_to_all | solution.py:28
  114.8 3.4 %all-to-all-start.8 = ((bf16[8,128,128]{1,2,0:T(8,128)(2,1)}), bf16[8,128,128]{1,2,0:T(8,128)(2,1)S(1)}, u32[]{:S(2)}, u32[]{:S(2)}) async-start(bf16[8,128,128]{1,2,0:T(8,128)(2,1)} %broadcast_in_dim.18), calls=%async_computation.8 | async-start | bytes 524288 | tf_op jit(solution)/shard_map/all_to_all | solution.py:28
  120.4 2.3 reshape.35
  122.7 2.2 convolution_bitcast_fusion.3
  124.9 2.3 reshape.33
  128.0 6.6 %all-to-all-start.6 = ((bf16[8,128,128]{1,2,0:T(8,128)(2,1)}), bf16[8,128,128]{1,2,0:T(8,128)(2,1)}, u32[]{:S(2)}, u32[]{:S(2)}) async-start(bf16[8,128,128]{1,2,0:T(8,128)(2,1)} %broadcast_in_dim.17), calls=%async_computation.6 | async-start | bytes 524288 | tf_op jit(solution)/shard_map/all_to_all | solution.py:28
  134.5 3.4 %constant_dynamic-slice_fusion.5 = (f32[1,512,128]{1,0,2:T(1,128)}, f32[1,512,128]{1,0,2:T(1,128)}, f32[1,512,128]{1,0,2:T(1,128)}, f32[1,512,128]{1,0,2:T(1,128)}) fusion(f32[2,512,128]{1,0,2:T(2,128)} %reshape.35, s32[]{:T(128)S(6)} %select_n.36, s32[]{:T(128)S(6)} %select_n.37, f32[2,512,128]{1,0,2:T(2,128)} %reshape.33), kind=kLoop, calls=%fused_computation.63 | loop fusion | bytes 2097160 | tf_op jit(solution)/shard_map/jit(dynamic_index_in_dim)/dynamic_slice | solution.py:63
  139.7 11.0 %collective-permute-start.1 = (f32[512,128]{1,0:T(8,128)}, f32[512,128]{1,0:T(8,128)S(1)}, u32[]{:S(2)}, u32[]{:S(2)}) collective-permute-start(f32[512,128]{1,0:T(8,128)} %bitcast.127), channel_id=1, source_target_pairs={{0,1},{1,0},{2,3},{3,2},{4,5},{5,4},{6,7},{7,6},{8,9},{9,8},{10,11... | collective-permute-start | bytes 786440 | tf_op jit(solution)/shard_map/ppermute | solution.py:31
  150.7 2.2 convolution_bitcast_fusion
  152.9 2.3 reshape.39
  158.9 3.0 %constant_dynamic-slice_fusion.1 = (f32[1,512,128]{1,0,2:T(1,128)S(1)}, f32[1,512,128]{1,0,2:T(1,128)S(1)}, f32[1,512,128]{1,0,2:T(1,128)S(1)}, f32[1,512,128]{1,0,2:T(1,128)}) fusion(f32[2,512,128]{1,0,2:T(2,128)} %reshape.39, s32[]{:T(128)S(6)} %select_n.36, s32[]{:T(128)S(6)} %select_n.37, f32[2,512,128]{1,0,2:T(2,128)S(1)} %reshape.37), kind=kLoop, calls=%fused_computation.59 | loop fusion | bytes 2097160 | tf_op jit(solution)/shard_map/jit(dynamic_index_in_dim)/dynamic_slice | solution.py:63
  165.6 2.4 collective-permute-start.3
  172.6 15.5 %collective-permute-start.2 = (bf16[512,128]{1,0:T(8,128)(2,1)S(1)}, bf16[512,128]{1,0:T(8,128)(2,1)S(1)}, u32[]{:S(2)}, u32[]{:S(2)}) collective-permute-start(bf16[512,128]{1,0:T(8,128)(2,1)S(1)} %get-tuple-element.9), channel_id=1, source_target_pairs={{384,0},{400,16},{416,32},{432,48},{448,64},{464,80},{480,96},{496... | collective-permute-start | bytes 393224 | tf_op jit(solution)/shard_map/ppermute | solution.py:14
  190.1 12.1 %collective-permute-start.6 = (bf16[512,128]{1,0:T(8,128)(2,1)S(1)}, bf16[512,128]{1,0:T(8,128)(2,1)S(1)}, u32[]{:S(2)}, u32[]{:S(2)}) collective-permute-start(bf16[512,128]{1,0:T(8,128)(2,1)S(1)} %get-tuple-element.10), channel_id=1, source_target_pairs={{384,0},{400,16},{416,32},{432,48},{448,64},{464,80},{480,96},{496... | collective-permute-start | bytes 393224 | tf_op jit(solution)/shard_map/ppermute | solution.py:14
  204.1 27.7 %collective-permute-done.8 = bf16[512,128]{1,0:T(8,128)(2,1)S(1)} collective-permute-done((bf16[512,128]{1,0:T(8,128)(2,1)S(1)}, bf16[512,128]{1,0:T(8,128)(2,1)S(1)}, u32[]{:S(2)}, u32[]{:S(2)}) %collective-permute-start.8) | collective-permute-done | bytes 131104 | tf_op jit(solution)/shard_map/ppermute | solution.py:14
  231.9 5.6 %collective-permute-done.6 = bf16[512,128]{1,0:T(8,128)(2,1)S(1)} collective-permute-done((bf16[512,128]{1,0:T(8,128)(2,1)S(1)}, bf16[512,128]{1,0:T(8,128)(2,1)S(1)}, u32[]{:S(2)}, u32[]{:S(2)}) %collective-permute-start.6) | collective-permute-done | bytes 131104 | tf_op jit(solution)/shard_map/ppermute | solution.py:14
  237.4 2.8 %collective-permute-done.4 = bf16[512,128]{1,0:T(8,128)(2,1)S(1)} collective-permute-done((bf16[512,128]{1,0:T(8,128)(2,1)S(1)}, bf16[512,128]{1,0:T(8,128)(2,1)S(1)}, u32[]{:S(2)}, u32[]{:S(2)}) %collective-permute-start.4) | collective-permute-done | bytes 131104 | tf_op jit(solution)/shard_map/ppermute | solution.py:14
  (60 shorter events, 45.6 us)
Async XLA Ops:
  5.8 7.6 %copy-start = (f32[1,512,512]{2,1,0:T(8,128)S(1)}, f32[1,512,512]{2,1,0:T(8,128)}, u32[]{:S(2)}) copy-start(f32[1,512,512]{2,1,0:T(8,128)} %param.3) | copy-start | bytes 3145732
  5.8 32.8 %all-to-all-start = ((bf16[8,128,1024]{2,1,0:T(8,128)(2,1)}), bf16[8,128,1024]{2,1,0:T(8,128)(2,1)S(1)}, u32[]{:S(2)}, u32[]{:S(2)}) async-start(bf16[8,128,1024]{2,1,0:T(8,128)(2,1)} %bitcast.120), calls=%async_computation | async-start | bytes 4194304 | tf_op jit(solution)/shard_map/all_to_all | solution.py:28
  14.3 6.8 %collective-permute-start = (bf16[512,512]{1,0:T(8,128)(2,1)}, bf16[512,512]{1,0:T(8,128)(2,1)}, u32[]{:S(2)}, u32[]{:S(2)}) collective-permute-start(bf16[512,512]{1,0:T(8,128)(2,1)} %bitcast_convert_fusion), channel_id=1, source_target_pairs={{0,1},{1,0},{2,3},{3,2},{4,5},{5,4},{6,7},{7,6},{8,9},{9,8},{10,11... | collective-permute-start | bytes 1572872 | tf_op jit(solution)/shard_map/ppermute | solution.py:31
  41.2 13.5 %all-to-all-start.1 = ((bf16[8,128,128]{1,2,0:T(8,128)(2,1)}), bf16[8,128,128]{1,2,0:T(8,128)(2,1)S(1)}, u32[]{:S(2)}, u32[]{:S(2)}) async-start(bf16[8,128,128]{1,2,0:T(8,128)(2,1)} %bitcast.125), calls=%async_computation.1 | async-start | bytes 524288 | tf_op jit(solution)/shard_map/all_to_all | solution.py:28
  54.7 11.8 %all-to-all-start.7 = ((bf16[8,128,128]{1,2,0:T(8,128)(2,1)}), bf16[8,128,128]{1,2,0:T(8,128)(2,1)}, u32[]{:S(2)}, u32[]{:S(2)}) async-start(bf16[8,128,128]{1,2,0:T(8,128)(2,1)} %bitcast.124), calls=%async_computation.7 | async-start | bytes 524288 | tf_op jit(solution)/shard_map/all_to_all | solution.py:28
  66.5 11.7 %all-to-all-start.5 = ((bf16[8,128,128]{1,2,0:T(8,128)(2,1)}), bf16[8,128,128]{1,2,0:T(8,128)(2,1)}, u32[]{:S(2)}, u32[]{:S(2)}) async-start(bf16[8,128,128]{1,2,0:T(8,128)(2,1)} %bitcast.122), calls=%async_computation.5 | async-start | bytes 524288 | tf_op jit(solution)/shard_map/all_to_all | solution.py:28
  78.2 11.0 %all-to-all-start.3 = ((bf16[8,128,128]{1,2,0:T(8,128)(2,1)}), bf16[8,128,128]{1,2,0:T(8,128)(2,1)S(1)}, u32[]{:S(2)}, u32[]{:S(2)}) async-start(bf16[8,128,128]{1,2,0:T(8,128)(2,1)} %bitcast.123), calls=%async_computation.3 | async-start | bytes 524288 | tf_op jit(solution)/shard_map/all_to_all | solution.py:28
  102.3 11.0 %all-to-all-start.2 = ((bf16[8,128,128]{1,2,0:T(8,128)(2,1)}), bf16[8,128,128]{1,2,0:T(8,128)(2,1)S(1)}, u32[]{:S(2)}, u32[]{:S(2)}) async-start(bf16[8,128,128]{1,2,0:T(8,128)(2,1)} %broadcast_in_dim.15), calls=%async_computation.2 | async-start | bytes 524288 | tf_op jit(solution)/shard_map/all_to_all | solution.py:28
  113.3 1.5 copy-start.5
  114.8 12.4 %all-to-all-start.8 = ((bf16[8,128,128]{1,2,0:T(8,128)(2,1)}), bf16[8,128,128]{1,2,0:T(8,128)(2,1)S(1)}, u32[]{:S(2)}, u32[]{:S(2)}) async-start(bf16[8,128,128]{1,2,0:T(8,128)(2,1)} %broadcast_in_dim.18), calls=%async_computation.8 | async-start | bytes 524288 | tf_op jit(solution)/shard_map/all_to_all | solution.py:28
  122.7 4.5 %copy-start.6 = (bf16[128,128]{0,1:T(8,128)(2,1)S(1)}, bf16[128,128]{0,1:T(8,128)(2,1)}, u32[]{:S(2)}) copy-start(bf16[128,128]{0,1:T(8,128)(2,1)} %get-tuple-element.25) | copy-start | bytes 98308
  127.2 12.6 %copy-start.4 = (bf16[8,128,128]{1,2,0:T(8,128)(2,1)}, bf16[8,128,128]{1,2,0:T(8,128)(2,1)S(1)}, u32[]{:S(2)}) copy-start(bf16[8,128,128]{1,2,0:T(8,128)(2,1)S(1)} %all-to-all-done.8) | copy-start | bytes 786436
  128.0 27.2 %all-to-all-start.6 = ((bf16[8,128,128]{1,2,0:T(8,128)(2,1)}), bf16[8,128,128]{1,2,0:T(8,128)(2,1)}, u32[]{:S(2)}, u32[]{:S(2)}) async-start(bf16[8,128,128]{1,2,0:T(8,128)(2,1)} %broadcast_in_dim.17), calls=%async_computation.6 | async-start | bytes 524288 | tf_op jit(solution)/shard_map/all_to_all | solution.py:28
  139.7 32.5 %collective-permute-start.1 = (f32[512,128]{1,0:T(8,128)}, f32[512,128]{1,0:T(8,128)S(1)}, u32[]{:S(2)}, u32[]{:S(2)}) collective-permute-start(f32[512,128]{1,0:T(8,128)} %bitcast.127), channel_id=1, source_target_pairs={{0,1},{1,0},{2,3},{3,2},{4,5},{5,4},{6,7},{7,6},{8,9},{9,8},{10,11... | collective-permute-start | bytes 786440 | tf_op jit(solution)/shard_map/ppermute | solution.py:31
  157.4 7.4 %copy-start.3 = (f32[1,512,128]{1,0,2:T(1,128)S(1)}, f32[1,512,128]{1,0,2:T(1,128)}, u32[]{:S(2)}) copy-start(f32[1,512,128]{1,0,2:T(1,128)} %get-tuple-element.18) | copy-start | bytes 786436
  158.9 11.8 %copy-start.2 = (f32[1,512,128]{1,0,2:T(1,128)S(1)}, f32[1,512,128]{1,0,2:T(1,128)}, u32[]{:S(2)}) copy-start(f32[1,512,128]{1,0,2:T(1,128)} %get-tuple-element.30) | copy-start | bytes 786436
  158.9 13.1 %copy-start.1 = (f32[1,512,128]{1,0,2:T(1,128)S(1)}, f32[1,512,128]{1,0,2:T(1,128)}, u32[]{:S(2)}) copy-start(f32[1,512,128]{1,0,2:T(1,128)} %get-tuple-element.17) | copy-start | bytes 786436
  162.8 9.5 %collective-permute-start.5 = (f32[512,128]{1,0:T(8,128)}, f32[512,128]{1,0:T(8,128)S(1)}, u32[]{:S(2)}, u32[]{:S(2)}) collective-permute-start(f32[512,128]{1,0:T(8,128)} %bitcast.19), channel_id=1, source_target_pairs={{0,1},{1,0},{2,3},{3,2},{4,5},{5,4},{6,7},{7,6},{8,9},{9,8},{10,11... | collective-permute-start | bytes 786440 | tf_op jit(solution)/shard_map/ppermute | solution.py:31
  165.6 6.7 %collective-permute-start.3 = (f32[512,128]{1,0:T(8,128)}, f32[512,128]{1,0:T(8,128)S(1)}, u32[]{:S(2)}, u32[]{:S(2)}) collective-permute-start(f32[512,128]{1,0:T(8,128)} %bitcast.14), channel_id=1, source_target_pairs={{0,1},{1,0},{2,3},{3,2},{4,5},{5,4},{6,7},{7,6},{8,9},{9,8},{10,11... | collective-permute-start | bytes 786440 | tf_op jit(solution)/shard_map/ppermute | solution.py:31
  168.8 3.6 %collective-permute-start.7 = (f32[512,128]{1,0:T(8,128)}, f32[512,128]{1,0:T(8,128)S(1)}, u32[]{:S(2)}, u32[]{:S(2)}) collective-permute-start(f32[512,128]{1,0:T(8,128)} %bitcast.24), channel_id=1, source_target_pairs={{0,1},{1,0},{2,3},{3,2},{4,5},{5,4},{6,7},{7,6},{8,9},{9,8},{10,11... | collective-permute-start | bytes 786440 | tf_op jit(solution)/shard_map/ppermute | solution.py:31
  172.6 31.5 %collective-permute-start.2 = (bf16[512,128]{1,0:T(8,128)(2,1)S(1)}, bf16[512,128]{1,0:T(8,128)(2,1)S(1)}, u32[]{:S(2)}, u32[]{:S(2)}) collective-permute-start(bf16[512,128]{1,0:T(8,128)(2,1)S(1)} %get-tuple-element.9), channel_id=1, source_target_pairs={{384,0},{400,16},{416,32},{432,48},{448,64},{464,80},{480,96},{496... | collective-permute-start | bytes 393224 | tf_op jit(solution)/shard_map/ppermute | solution.py:14
  188.1 43.7 %collective-permute-start.8 = (bf16[512,128]{1,0:T(8,128)(2,1)S(1)}, bf16[512,128]{1,0:T(8,128)(2,1)S(1)}, u32[]{:S(2)}, u32[]{:S(2)}) collective-permute-start(bf16[512,128]{1,0:T(8,128)(2,1)S(1)} %get-tuple-element.12), channel_id=1, source_target_pairs={{384,0},{400,16},{416,32},{432,48},{448,64},{464,80},{480,96},{496... | collective-permute-start | bytes 393224 | tf_op jit(solution)/shard_map/ppermute | solution.py:14
  190.1 47.4 %collective-permute-start.6 = (bf16[512,128]{1,0:T(8,128)(2,1)S(1)}, bf16[512,128]{1,0:T(8,128)(2,1)S(1)}, u32[]{:S(2)}, u32[]{:S(2)}) collective-permute-start(bf16[512,128]{1,0:T(8,128)(2,1)S(1)} %get-tuple-element.10), channel_id=1, source_target_pairs={{384,0},{400,16},{416,32},{432,48},{448,64},{464,80},{480,96},{496... | collective-permute-start | bytes 393224 | tf_op jit(solution)/shard_map/ppermute | solution.py:14
  202.2 38.1 %collective-permute-start.4 = (bf16[512,128]{1,0:T(8,128)(2,1)S(1)}, bf16[512,128]{1,0:T(8,128)(2,1)S(1)}, u32[]{:S(2)}, u32[]{:S(2)}) collective-permute-start(bf16[512,128]{1,0:T(8,128)(2,1)S(1)} %get-tuple-element.11), channel_id=1, source_target_pairs={{384,0},{400,16},{416,32},{432,48},{448,64},{464,80},{480,96},{496... | collective-permute-start | bytes 393224 | tf_op jit(solution)/shard_map/ppermute | solution.py:14

commit v2 on v0

v2 whole, which is shorter than its diff:
```python
import functools

import jax
import jax.numpy as jnp
from jax import lax
from jax.experimental import pallas as pl
from jax.experimental.pallas import tpu as pltpu
from jax.sharding import PartitionSpec as P

D = 8192
STEP = 3
HALVES = 2
SCALE = 1.0 / D**0.5

VMEM = pl.BlockSpec(memory_space=pltpu.VMEM)
ANY = pl.BlockSpec(memory_space=pl.ANY)
F32 = jnp.float32
BF16 = jnp.bfloat16


def call(kernel, name, outs, ins, spec=VMEM, aliases=None):
    return pl.pallas_call(
        kernel,
        name=name,
        out_shape=[jax.ShapeDtypeStruct(s, d) for s, d in outs],
        in_specs=list(ins),
        out_specs=[spec] * len(outs),
        input_output_aliases=aliases or {},
        compiler_params=pltpu.CompilerParams(vmem_limit_bytes=8 * 1024 * 1024),
        cost_estimate=pl.CostEstimate(flops=1_000_000, bytes_accessed=1_000_000, transcendentals=0),
    )


def round_kernel(master, working):
    working[...] = master[...].astype(BF16)


def block_kernel(features, _, blocks):
    core = lax.rem(lax.axis_index("fsdp"), 2)
    chips, _, _, rows = blocks.shape
    for q in range(chips):
        for h, half in enumerate((core, 1 - core)):
            start = pl.multiple_of(q * 2 * rows + half * rows, rows)
            blocks[q, h] = features[:, pl.ds(start, rows)]


def after_kernel(*_):
    pass


def keys_kernel(blocks, own, peer, out):
    chips, _, count, rows = blocks.shape
    first = blocks[:, 0].reshape(chips * count, rows)
    second = blocks[:, 1].reshape(chips * count, rows)
    for c in range(0, own.shape[1], 256):
        part = slice(c, c + 256)
        total = jnp.dot(first, own[:, part], preferred_element_type=F32)
        total += jnp.dot(second, peer[:, part], preferred_element_type=F32)
        out[:, :, part] = (total * SCALE).astype(BF16).reshape(chips, count, 256)


def error_kernel(parts, targets, out):
    for c in range(0, out.shape[2], 128):
        part = slice(c, c + 128)
        keys = parts[0, :, part].astype(F32)
        for q in range(1, parts.shape[0]):
            keys += parts[q, :, part].astype(F32)
        error = (keys - targets[:, part].astype(F32)).astype(BF16)
        for q in range(out.shape[0]):
            out[q, :, part] = error


def grad_kernel(k, start, stop, blocks, errors, *rest):
    chips, _, count, rows = blocks.shape
    grad = lax.dot_general(
        blocks[:, k].reshape(chips * count, rows),
        errors[:, :, start:stop].reshape(chips * count, stop - start),
        (((0,), (0,)), ((), ())),
        preferred_element_type=F32,
    )
    rest[-1][...] = grad.astype(rest[-1].dtype)


def step_kernel(start, stop, kept, given, master, stepped, sent):
    new = master[:, start:stop] - (0.5 * SCALE) * (kept[...] + given[...].astype(F32))
    stepped[...] = new
    sent[...] = new.astype(BF16)


def average_kernel(chunks, *refs):
    out = refs[-1]
    for i, (start, stop) in enumerate(chunks):
        out[:, start:stop] = 0.5 * (refs[2 * i][...] + refs[2 * i + 1][...].astype(F32))


def from_behind(block, axis, distance):
    devices = range(lax.axis_size(axis))
    route = [((i - distance) % len(devices), i) for i in devices]
    return lax.ppermute(block, axis, route)


def body(master, features, targets):
    levels = lax.axis_size("rep").bit_length() - 1
    hop = 2 ** (STEP % levels)
    size = lax.axis_size("fsdp")
    chips = size // 2
    groups = [list(range(c, size, 2)) for c in range(2)]
    swap_route = [(i, i ^ 1) for i in range(size)]

    def exchange(blocks):
        return lax.all_to_all(blocks, "fsdp", 0, 0, axis_index_groups=groups)

    def swap(block):
        return lax.ppermute(block, "fsdp", swap_route)

    master, tokens, targets = master[0], features[0], targets[0]
    rows, width = master.shape
    count = tokens.shape[0]
    part = width // HALVES
    chunks = [(h * part, (h + 1) * part) for h in range(HALVES)]

    (working,) = call(round_kernel, "round", [((rows, width), BF16)], [VMEM])(master)
    peer = swap(working)
    shape = (chips, 2, count, rows)
    (blocks,) = call(block_kernel, "block", [(shape, BF16)], [VMEM, ANY])(tokens, working)
    (blocks,) = call(after_kernel, "after", [(shape, BF16)], [ANY] * 2, ANY, {0: 0})(blocks, peer)
    blocks = exchange(blocks)

    shape = (chips, count, width)
    (partial,) = call(keys_kernel, "keys", [(shape, BF16)], [VMEM] * 3)(blocks, working, peer)
    (error,) = call(error_kernel, "error", [(shape, BF16)], [VMEM] * 2)(exchange(partial), targets)
    errors = exchange(error)

    results, given, after = [], [], []
    for h, (start, stop) in enumerate(chunks):
        (term,) = call(
            functools.partial(grad_kernel, 1, start, stop),
            f"given_{h}",
            [((rows, part), BF16)],
            [VMEM] * 2 + [ANY] * len(after),
        )(blocks, errors, *after)
        after = [term]
        given.append(swap(term))
    for h, (start, stop) in enumerate(chunks):
        (kept,) = call(
            functools.partial(grad_kernel, 0, start, stop),
            f"kept_{h}",
            [((rows, part), F32)],
            [VMEM] * 2 + [ANY] * len(after),
        )(blocks, errors, *after)
        stepped, sent = call(
            functools.partial(step_kernel, start, stop),
            f"step_{h}",
            [((rows, part), F32), ((rows, part), BF16)],
            [VMEM] * 3,
        )(kept, given[h], master)
        after = [kept]
        results += [stepped, from_behind(sent, "rep", hop)]
    (updated,) = call(
        functools.partial(average_kernel, chunks),
        "average",
        [((rows, width), F32)],
        [VMEM] * len(results),
    )(*results)
    return updated[None]


def solution(mesh):
    return jax.shard_map(
        body,
        mesh=mesh,
        in_specs=(P("rep", "fsdp", None), P("rep", "fsdp", None), P("rep", "fsdp", None)),
        out_specs=P("rep", "fsdp", None),
        check_vma=False,
    )
```

time: 294 us -> 150 us (0.51)
  the two profiles are of different devices: /device:TPU:8 before, /device:TPU:34 now
where the time goes in v2:
time: 150 us; the launch traced here: 149 us
  blocking collectives  72.8 us (49%)
  waiting for transfers between devices  45.1 us (30%)
  starting transfers between devices  23 us (15%)
  Pallas kernels  4.84 us (3%)
  local copies, waits for them, and re-layouts  3.53 us (2%)
    all_to_all x3, blocking collectives, exchange(): return lax.all_to_all(blocks, 'fsdp', 0, 0, axis_index_groups=groups)  72.8 us
    ppermute x2, waiting for transfers between devices, from_behind(): return lax.ppermute(block, axis, route)  44.9 us
    ppermute x2, starting transfers between devices, from_behind(): return lax.ppermute(block, axis, route)  16.7 us
    ppermute x3, starting transfers between devices, swap(): return lax.ppermute(block, 'fsdp', swap_route)  6.25 us
    unnamed x8, local copies, waits for them, and re-layouts  3.53 us
  transfers between devices with their start and end apart: 5, of which 3 were waited for; matrix products, arithmetic and copies ran while one was open for 0% of the time, Pallas kernels for 1%

profile of v2, /device:TPU:34, one launch (start us, length us, event | category | flops | bytes accessed | tf_op | source)
XLA Modules:
  0.0 149.4 jit_solution(11999776966516662931)
XLA Ops:
  0.0 0.0 copy-start
  0.0 1.2 copy-done
  1.2 0.1 round.1._.own
  1.3 1.9 %collective-permute-start = (bf16[512,512]{1,0:T(8,128)(2,1)S(1)}, bf16[512,512]{1,0:T(8,128)(2,1)S(1)}, u32[]{:S(2)}, u32[]{:S(2)}) collective-permute-start(bf16[512,512]{1,0:T(8,128)(2,1)S(1)} %round.1._.own), channel_id=1, source_target_pairs={{0,1},{1,0},{2,3},{3,2},{4,5},{5,4},{6,7},{7,6},{8,9},{9,8},{10,11... | collective-permute-start | bytes 1572872 | tf_op jit(solution)/shard_map/ppermute | solution.py:114
  3.2 0.0 copy-start.2
  3.2 1.6 %copy-done.2 = bf16[1,128,8192]{2,1,0:T(8,128)(2,1)S(1)} copy-done((bf16[1,128,8192]{2,1,0:T(8,128)(2,1)S(1)}, bf16[1,128,8192]{2,1,0:T(8,128)(2,1)}, u32[]{:S(2)}) %copy-start.2) | copy-done | bytes 2097176
  4.8 0.1 block.1.__0_
  4.9 0.1 collective-permute-done.__1_.peer
  5.1 34.8 %all_to_all.15.blocks = bf16[8,2,128,512]{3,2,1,0:T(8,128)(2,1)S(1)} all-to-all(bf16[8,2,128,512]{3,2,1,0:T(8,128)(2,1)S(1)} %after.1), channel_id=1, replica_groups={{0,2,4,6,8,10,12,14},{1,3,5,7,9,11,13,15},{16,18,20,22,24,26,28,30},{17..., dimensions={0} | all-to-all | bytes 4194304 | tf_op jit(solution)/shard_map/all_to_all | solution.py:111
  39.9 1.2 keys.1
  41.1 0.0 copy-start.3
  41.2 19.5 %all_to_all.16.parts = bf16[8,128,512]{2,1,0:T(8,128)(2,1)S(1)} all-to-all(bf16[8,128,512]{2,1,0:T(8,128)(2,1)S(1)} %keys.1), channel_id=1, replica_groups={{0,2,4,6,8,10,12,14},{1,3,5,7,9,11,13,15},{16,18,20,22,24,26,28,30},{17..., dimensions={0} | all-to-all | bytes 2097152 | tf_op jit(solution)/shard_map/all_to_all | solution.py:111
  60.6 0.0 copy-done.3
  60.6 0.2 error.1
  60.9 18.5 %all_to_all.17.errors = bf16[8,128,512]{2,1,0:T(8,128)(2,1)S(1)} all-to-all(bf16[8,128,512]{2,1,0:T(8,128)(2,1)S(1)} %error.1), channel_id=1, replica_groups={{0,2,4,6,8,10,12,14},{1,3,5,7,9,11,13,15},{16,18,20,22,24,26,28,30},{17..., dimensions={0} | all-to-all | bytes 2097152 | tf_op jit(solution)/shard_map/all_to_all | solution.py:111
  79.4 0.5 given_0.1.rest_0_
  79.9 0.5 given_1.1.rest_0_
  80.4 1.9 %collective-permute-start.3 = (bf16[512,256]{1,0:T(8,128)(2,1)S(1)}, bf16[512,256]{1,0:T(8,128)(2,1)S(1)}, u32[]{:S(2)}, u32[]{:S(2)}) collective-permute-start(bf16[512,256]{1,0:T(8,128)(2,1)S(1)} %given_1.1.rest_0_), channel_id=1, source_target_pairs={{0,1},{1,0},{2,3},{3,2},{4,5},{5,4},{6,7},{7,6},{8,9},{9,8},{10,11... | collective-permute-start | bytes 786440 | tf_op jit(solution)/shard_map/ppermute | solution.py:114
  82.3 2.4 %collective-permute-start.1 = (bf16[512,256]{1,0:T(8,128)(2,1)S(1)}, bf16[512,256]{1,0:T(8,128)(2,1)S(1)}, u32[]{:S(2)}, u32[]{:S(2)}) collective-permute-start(bf16[512,256]{1,0:T(8,128)(2,1)S(1)} %given_0.1.rest_0_), channel_id=1, source_target_pairs={{0,1},{1,0},{2,3},{3,2},{4,5},{5,4},{6,7},{7,6},{8,9},{9,8},{10,11... | collective-permute-start | bytes 786440 | tf_op jit(solution)/shard_map/ppermute | solution.py:114
  84.7 0.5 kept_0.1.kept.rest_0_
  85.2 0.0 copy-start.1
  85.2 0.5 kept_1.1.kept
  85.7 0.0 collective-permute-done.3.given
  85.7 0.7 copy-done.1
  86.4 0.1 step_1.1
  86.5 14.8 %collective-permute-start.4 = (bf16[512,256]{1,0:T(8,128)(2,1)S(1)}, bf16[512,256]{1,0:T(8,128)(2,1)S(1)}, u32[]{:S(2)}, u32[]{:S(2)}) collective-permute-start(bf16[512,256]{1,0:T(8,128)(2,1)S(1)} %get-tuple-element.12), channel_id=1, source_target_pairs={{384,0},{400,16},{416,32},{432,48},{448,64},{464,80},{480,96},{496... | collective-permute-start | bytes 786440 | tf_op jit(solution)/shard_map/ppermute | solution.py:99
  101.4 0.0 collective-permute-done.1.given
  101.4 0.1 step_0.1
  101.5 1.9 %collective-permute-start.2 = (bf16[512,256]{1,0:T(8,128)(2,1)S(1)}, bf16[512,256]{1,0:T(8,128)(2,1)S(1)}, u32[]{:S(2)}, u32[]{:S(2)}) collective-permute-start(bf16[512,256]{1,0:T(8,128)(2,1)S(1)} %get-tuple-element.10), channel_id=1, source_target_pairs={{384,0},{400,16},{416,32},{432,48},{448,64},{464,80},{480,96},{496... | collective-permute-start | bytes 786440 | tf_op jit(solution)/shard_map/ppermute | solution.py:99
  103.4 35.7 %collective-permute-done.4.refs_3_ = bf16[512,256]{1,0:T(8,128)(2,1)S(1)} collective-permute-done((bf16[512,256]{1,0:T(8,128)(2,1)S(1)}, bf16[512,256]{1,0:T(8,128)(2,1)S(1)}, u32[]{:S(2)}, u32[]{:S(2)}) %collective-permute-start.4) | collective-permute-done | bytes 262176 | tf_op jit(solution)/shard_map/ppermute | solution.py:99
  139.1 9.2 %collective-permute-done.2.refs_1_ = bf16[512,256]{1,0:T(8,128)(2,1)S(1)} collective-permute-done((bf16[512,256]{1,0:T(8,128)(2,1)S(1)}, bf16[512,256]{1,0:T(8,128)(2,1)S(1)}, u32[]{:S(2)}, u32[]{:S(2)}) %collective-permute-start.2) | collective-permute-done | bytes 262176 | tf_op jit(solution)/shard_map/ppermute | solution.py:99
  148.3 1.1 average.1
  (1 shorter events, 0.0 us)
Async XLA Ops:
  0.0 1.2 copy-start
  1.3 3.8 %collective-permute-start = (bf16[512,512]{1,0:T(8,128)(2,1)S(1)}, bf16[512,512]{1,0:T(8,128)(2,1)S(1)}, u32[]{:S(2)}, u32[]{:S(2)}) collective-permute-start(bf16[512,512]{1,0:T(8,128)(2,1)S(1)} %round.1._.own), channel_id=1, source_target_pairs={{0,1},{1,0},{2,3},{3,2},{4,5},{5,4},{6,7},{7,6},{8,9},{9,8},{10,11... | collective-permute-start | bytes 1572872 | tf_op jit(solution)/shard_map/ppermute | solution.py:114
  3.2 1.6 %copy-start.2 = (bf16[1,128,8192]{2,1,0:T(8,128)(2,1)S(1)}, bf16[1,128,8192]{2,1,0:T(8,128)(2,1)}, u32[]{:S(2)}) copy-start(bf16[1,128,8192]{2,1,0:T(8,128)(2,1)} %param.4) | copy-start | bytes 6291460
  41.1 19.5 %copy-start.3 = (bf16[1,128,512]{2,1,0:T(8,128)(2,1)S(1)}, bf16[1,128,512]{2,1,0:T(8,128)(2,1)}, u32[]{:S(2)}) copy-start(bf16[1,128,512]{2,1,0:T(8,128)(2,1)} %param.5) | copy-start | bytes 393220
  80.4 5.3 %collective-permute-start.3 = (bf16[512,256]{1,0:T(8,128)(2,1)S(1)}, bf16[512,256]{1,0:T(8,128)(2,1)S(1)}, u32[]{:S(2)}, u32[]{:S(2)}) collective-permute-start(bf16[512,256]{1,0:T(8,128)(2,1)S(1)} %given_1.1.rest_0_), channel_id=1, source_target_pairs={{0,1},{1,0},{2,3},{3,2},{4,5},{5,4},{6,7},{7,6},{8,9},{9,8},{10,11... | collective-permute-start | bytes 786440 | tf_op jit(solution)/shard_map/ppermute | solution.py:114
  82.3 19.1 %collective-permute-start.1 = (bf16[512,256]{1,0:T(8,128)(2,1)S(1)}, bf16[512,256]{1,0:T(8,128)(2,1)S(1)}, u32[]{:S(2)}, u32[]{:S(2)}) collective-permute-start(bf16[512,256]{1,0:T(8,128)(2,1)S(1)} %given_0.1.rest_0_), channel_id=1, source_target_pairs={{0,1},{1,0},{2,3},{3,2},{4,5},{5,4},{6,7},{7,6},{8,9},{9,8},{10,11... | collective-permute-start | bytes 786440 | tf_op jit(solution)/shard_map/ppermute | solution.py:114
  85.2 1.2 copy-start.1
  86.5 52.5 %collective-permute-start.4 = (bf16[512,256]{1,0:T(8,128)(2,1)S(1)}, bf16[512,256]{1,0:T(8,128)(2,1)S(1)}, u32[]{:S(2)}, u32[]{:S(2)}) collective-permute-start(bf16[512,256]{1,0:T(8,128)(2,1)S(1)} %get-tuple-element.12), channel_id=1, source_target_pairs={{384,0},{400,16},{416,32},{432,48},{448,64},{464,80},{480,96},{496... | collective-permute-start | bytes 786440 | tf_op jit(solution)/shard_map/ppermute | solution.py:99
  101.5 46.8 %collective-permute-start.2 = (bf16[512,256]{1,0:T(8,128)(2,1)S(1)}, bf16[512,256]{1,0:T(8,128)(2,1)S(1)}, u32[]{:S(2)}, u32[]{:S(2)}) collective-permute-start(bf16[512,256]{1,0:T(8,128)(2,1)S(1)} %get-tuple-element.10), channel_id=1, source_target_pairs={{384,0},{400,16},{416,32},{432,48},{448,64},{464,80},{480,96},{496... | collective-permute-start | bytes 786440 | tf_op jit(solution)/shard_map/ppermute | solution.py:99

commit v3 on v2

v3 whole, which is shorter than its diff:
```python
import functools

import jax
import jax.numpy as jnp
from jax import lax
from jax.experimental import pallas as pl
from jax.experimental.pallas import tpu as pltpu
from jax.sharding import PartitionSpec as P

D = 8192
STEP = 3
PIECES = (256, 256)
SIDE = 4
SCALE = 1.0 / D**0.5

VMEM = pl.BlockSpec(memory_space=pltpu.VMEM)
ANY = pl.BlockSpec(memory_space=pl.ANY)
F32 = jnp.float32
BF16 = jnp.bfloat16


def call(kernel, name, outs, ins, scratch=()):
    return pl.pallas_call(
        kernel,
        name=name,
        out_shape=[jax.ShapeDtypeStruct(s, d) for s, d in outs],
        in_specs=list(ins),
        out_specs=[VMEM] * len(outs),
        scratch_shapes=list(scratch),
        compiler_params=pltpu.CompilerParams(vmem_limit_bytes=8 * 1024 * 1024),
        cost_estimate=pl.CostEstimate(flops=1_000_000, bytes_accessed=1_000_000, transcendentals=0),
    )


def round_kernel(master, working):
    working[...] = master[...].astype(BF16)


def block_kernel(features, blocks):
    mine = lax.rem(lax.axis_index("fsdp"), SIDE)
    ring, _, _, rows = blocks.shape
    for k in range(SIDE):
        for y in range(ring):
            start = pl.multiple_of((y * SIDE + (mine ^ k)) * rows, rows)
            blocks[y, k] = features[:, pl.ds(start, rows)]


def keys_kernel(blocks, *refs):
    *sources, out, working, sem = refs
    ring, _, count, rows = blocks.shape
    copies = [
        pltpu.make_async_copy(source, working.at[k], sem.at[k]) for k, source in enumerate(sources)
    ]
    for copy in copies:
        copy.start()
    for copy in copies:
        copy.wait()
    for c in range(0, out.shape[2], 256):
        part = slice(c, c + 256)
        total = sum(
            jnp.dot(
                blocks[:, k].reshape(ring * count, rows),
                working[k, :, part],
                preferred_element_type=F32,
            )
            for k in range(SIDE)
        )
        out[:, :, part] = (total * SCALE).astype(BF16).reshape(ring, count, 256)


def error_kernel(parts, targets, out):
    for c in range(0, out.shape[2], 128):
        part = slice(c, c + 128)
        keys = parts[0, :, part].astype(F32)
        for q in range(1, parts.shape[0]):
            keys += parts[q, :, part].astype(F32)
        error = (keys - targets[:, part].astype(F32)).astype(BF16)
        for q in range(out.shape[0]):
            out[q, :, part] = error


def term(blocks, errors, k, start, stop):
    ring, _, count, rows = blocks.shape
    return lax.dot_general(
        blocks[:, k].reshape(ring * count, rows),
        errors[:, :, start:stop].reshape(ring * count, stop - start),
        (((0,), (0,)), ((), ())),
        preferred_element_type=F32,
    )


def given_kernel(start, stop, blocks, errors, out):
    for i, k in enumerate((3, 1)):
        out[i] = term(blocks, errors, k, start, stop).astype(BF16)


def kept_kernel(start, stop, blocks, errors, _, across, own):
    across[...] = term(blocks, errors, 2, start, stop)
    own[...] = term(blocks, errors, 0, start, stop)


def across_kernel(kept, given, out):
    out[...] = (kept[...] + given[0].astype(F32)).astype(BF16)


def step_kernel(start, stop, kept, given, crossed, master, stepped, sent):
    grad = kept[...] + given[1].astype(F32) + crossed[...].astype(F32)
    new = master[:, start:stop] - (0.5 * SCALE) * grad
    stepped[...] = new
    sent[...] = new.astype(BF16)


def average_kernel(chunks, *refs):
    out = refs[-1]
    for i, (start, stop) in enumerate(chunks):
        out[:, start:stop] = 0.5 * (refs[2 * i][...] + refs[2 * i + 1][...].astype(F32))


def from_behind(block, axis, distance):
    devices = range(lax.axis_size(axis))
    route = [((i - distance) % len(devices), i) for i in devices]
    return lax.ppermute(block, axis, route)


def body(master, features, targets):
    levels = lax.axis_size("rep").bit_length() - 1
    hop = 2 ** (STEP % levels)
    size = lax.axis_size("fsdp")
    ring = size // SIDE
    groups = [list(range(k, size, SIDE)) for k in range(SIDE)]

    def exchange(blocks):
        return lax.all_to_all(blocks, "fsdp", 0, 0, axis_index_groups=groups)

    def swap(block, k):
        return lax.ppermute(block, "fsdp", [(i, i ^ k) for i in range(size)])

    master, tokens, targets = master[0], features[0], targets[0]
    rows, width = master.shape
    count = tokens.shape[0]
    edges = [sum(PIECES[:h]) for h in range(len(PIECES) + 1)]
    chunks = list(zip(edges[:-1], edges[1:]))

    (working,) = call(round_kernel, "round", [((rows, width), BF16)], [VMEM])(master)
    beside = swap(working, 1)
    across = swap(working, 2)
    working = [working, beside, across, swap(across, 1)]
    shape = (ring, SIDE, count, rows)
    (blocks,) = call(block_kernel, "block", [(shape, BF16)], [VMEM])(tokens)
    blocks = exchange(blocks)

    shape = (ring, count, width)
    (partial,) = call(
        keys_kernel,
        "keys",
        [(shape, BF16)],
        [VMEM] + [ANY] * SIDE,
        scratch=[pltpu.VMEM((SIDE, rows, width), BF16), pltpu.SemaphoreType.DMA((SIDE,))],
    )(blocks, *working)
    (error,) = call(error_kernel, "error", [(shape, BF16)], [VMEM] * 2)(exchange(partial), targets)
    errors = exchange(error)

    results = []
    for h, (start, stop) in enumerate(chunks):
        half = (rows, stop - start)
        (given,) = call(
            functools.partial(given_kernel, start, stop),
            f"given_{h}",
            [((2, *half), BF16)],
            [VMEM] * 2,
        )(blocks, errors)
        across, kept = call(
            functools.partial(kept_kernel, start, stop),
            f"kept_{h}",
            [(half, F32)] * 2,
            [VMEM] * 2 + [ANY],
        )(blocks, errors, given)
        given = swap(given, 1)
        (across,) = call(across_kernel, f"across_{h}", [(half, BF16)], [VMEM] * 2)(across, given)
        stepped, sent = call(
            functools.partial(step_kernel, start, stop),
            f"step_{h}",
            [(half, F32), (half, BF16)],
            [VMEM] * 4,
        )(kept, given, swap(across, 2), master)
        results += [stepped, from_behind(sent, "rep", hop)]
    (updated,) = call(
        functools.partial(average_kernel, chunks),
        "average",
        [((rows, width), F32)],
        [VMEM] * len(results),
    )(*results)
    return updated[None]


def solution(mesh):
    return jax.shard_map(
        body,
        mesh=mesh,
        in_specs=(P("rep", "fsdp", None), P("rep", "fsdp", None), P("rep", "fsdp", None)),
        out_specs=P("rep", "fsdp", None),
        check_vma=False,
    )
```

time: 150 us -> 142 us (0.947)
  the two profiles are of different devices: /device:TPU:34 before, /device:TPU:32 now
where the time goes in v3:
time: 142 us; the launch traced here: 141 us
  waiting for transfers between devices  58.9 us (41%)
  starting transfers between devices  45 us (32%)
  blocking collectives  21.4 us (15%)
  local copies, waits for them, and re-layouts  10.3 us (7%)
  Pallas kernels  5.08 us (4%)
    ppermute x2, waiting for transfers between devices, from_behind(): return lax.ppermute(block, axis, route)  40.6 us
    all_to_all x2, blocking collectives, exchange(): return lax.all_to_all(blocks, 'fsdp', 0, 0, axis_index_groups=groups)  21.4 us
    ppermute x7, starting transfers between devices, swap(): return lax.ppermute(block, 'fsdp', [(i, i ^ k) for i in range(size)])  20.4 us
    ppermute x2, starting transfers between devices, from_behind(): return lax.ppermute(block, axis, route)  20 us
    ppermute x7, waiting for transfers between devices, swap(): return lax.ppermute(block, 'fsdp', [(i, i ^ k) for i in range(size)])  13.4 us
    unnamed x24, local copies, waits for them, and re-layouts  10.3 us
    all_to_all x1, waiting for transfers between devices, exchange(): return lax.all_to_all(blocks, 'fsdp', 0, 0, axis_index_groups=groups)  4.89 us
    all_to_all x1, starting transfers between devices, exchange(): return lax.all_to_all(blocks, 'fsdp', 0, 0, axis_index_groups=groups)  4.59 us
  transfers between devices with their start and end apart: 10, of which 6 were waited for; matrix products, arithmetic and copies ran while one was open for 0% of the time, Pallas kernels for 1%

profile of v3, /device:TPU:32, one launch (start us, length us, event | category | flops | bytes accessed | tf_op | source)
XLA Modules:
  0.0 140.9 jit_solution(14009569440498935459)
XLA Ops:
  0.0 1.6 %copy-done.4 = bf16[1,128,8192]{2,1,0:T(8,128)(2,1)S(1)} copy-done((bf16[1,128,8192]{2,1,0:T(8,128)(2,1)S(1)}, bf16[1,128,8192]{2,1,0:T(8,128)(2,1)}, u32[]{:S(2)}) %copy-start.4) | copy-done | bytes 2097176
  1.8 1.3 copy-done.1
  3.1 4.6 %all-to-all-start = ((bf16[4,4,128,512]{3,2,1,0:T(8,128)(2,1)}), bf16[4,4,128,512]{3,2,1,0:T(8,128)(2,1)S(1)}, u32[]{:S(2)}, u32[]{:S(2)}) async-start(bf16[4,4,128,512]{3,2,1,0:T(8,128)(2,1)} %copy-done.1), calls=%async_computation | async-start | bytes 4194304 | tf_op jit(solution)/shard_map/all_to_all | solution.py:133
  7.7 4.9 %collective-permute-start.1 = (bf16[512,512]{1,0:T(8,128)(2,1)S(1)}, bf16[512,512]{1,0:T(8,128)(2,1)S(1)}, u32[]{:S(2)}, u32[]{:S(2)}) collective-permute-start(bf16[512,512]{1,0:T(8,128)(2,1)S(1)} %round.1.refs_0_), channel_id=1, source_target_pairs={{0,2},{1,3},{2,0},{3,1},{4,6},{5,7},{6,4},{7,5},{8,10},{9,11},{10,... | collective-permute-start | bytes 1572872 | tf_op jit(solution)/shard_map/ppermute | solution.py:136
  12.7 1.9 %collective-permute-start = (bf16[512,512]{1,0:T(8,128)(2,1)S(1)}, bf16[512,512]{1,0:T(8,128)(2,1)S(1)}, u32[]{:S(2)}, u32[]{:S(2)}) collective-permute-start(bf16[512,512]{1,0:T(8,128)(2,1)S(1)} %round.1.refs_0_), channel_id=1, source_target_pairs={{0,1},{1,0},{2,3},{3,2},{4,5},{5,4},{6,7},{7,6},{8,9},{9,8},{10,11... | collective-permute-start | bytes 1572872 | tf_op jit(solution)/shard_map/ppermute | solution.py:136
  14.6 0.8 copy-done.2
  15.4 9.1 %collective-permute-done.1.refs_2_ = bf16[512,512]{1,0:T(8,128)(2,1)S(1)} collective-permute-done((bf16[512,512]{1,0:T(8,128)(2,1)S(1)}, bf16[512,512]{1,0:T(8,128)(2,1)S(1)}, u32[]{:S(2)}, u32[]{:S(2)}) %collective-permute-start.1) | collective-permute-done | bytes 524320 | tf_op jit(solution)/shard_map/ppermute | solution.py:136
  24.5 1.9 %collective-permute-start.2 = (bf16[512,512]{1,0:T(8,128)(2,1)S(1)}, bf16[512,512]{1,0:T(8,128)(2,1)S(1)}, u32[]{:S(2)}, u32[]{:S(2)}) collective-permute-start(bf16[512,512]{1,0:T(8,128)(2,1)S(1)} %collective-permute-done.1.refs_2_), channel_id=1, source_target_pairs={{0,1},{1,0},{2,3},{3,2},{4,5},{5,4},{6,7},{7,6},{8,9},{9,8},{10,11... | collective-permute-start | bytes 1572872 | tf_op jit(solution)/shard_map/ppermute | solution.py:136
  26.5 0.8 copy-done.5
  27.2 0.8 copy-done.7
  28.3 0.8 copy-done.9
  29.1 4.9 %all-to-all-done.blocks = bf16[4,4,128,512]{3,2,1,0:T(8,128)(2,1)S(1)} async-done(((bf16[4,4,128,512]{3,2,1,0:T(8,128)(2,1)}), bf16[4,4,128,512]{3,2,1,0:T(8,128)(2,1)S(1)}, u32[]{:S(2)}, u32[]{:S(2)}) %all-to-all-start) | async-done | bytes 2097184 | tf_op jit(solution)/shard_map/all_to_all | solution.py:133
  34.0 1.0 copy-done.3
  35.1 1.0 copy-done.6
  36.1 1.0 copy-done.8
  37.1 1.0 copy-done.10
  38.2 1.4 %keys.1 = bf16[4,128,512]{2,1,0:T(8,128)(2,1)S(1)} custom-call(bf16[4,4,128,512]{3,2,1,0:T(8,128)(2,1)S(1)} %all-to-all-done.blocks, bf16[512,512]{1,0:T(8,128)(2,1)S(1)} %copy-done.3, bf16[512,512]{1,0:T(8,128)(2,1)S(1)} %copy-done.8, bf16[512,512]{1,0:T(8,128)(2,1)S(1)} %copy-done.6, bf16[512,512]{1,0:T(8,128)(2,1)S(1)} %copy-done.10), custom_call_target="tpu_custom_call" | custom-call | flops 1000000 | bytes 1000000 | tf_op jit(solution)/shard_map/keys/pallas_call | solution.py:153
  39.6 11.0 %all_to_all.15.parts = bf16[4,128,512]{2,1,0:T(8,128)(2,1)S(1)} all-to-all(bf16[4,128,512]{2,1,0:T(8,128)(2,1)S(1)} %keys.1), channel_id=1, replica_groups={{0,4,8,12},{1,5,9,13},{2,6,10,14},{3,7,11,15},{16,20,24,28},{17,21,25,2..., dimensions={0} | all-to-all | bytes 1048576 | tf_op jit(solution)/shard_map/all_to_all | solution.py:133
  50.7 10.5 %all_to_all.16.errors = bf16[4,128,512]{2,1,0:T(8,128)(2,1)S(1)} all-to-all(bf16[4,128,512]{2,1,0:T(8,128)(2,1)S(1)} %error.1), channel_id=1, replica_groups={{0,4,8,12},{1,5,9,13},{2,6,10,14},{3,7,11,15},{16,20,24,28},{17,21,25,2..., dimensions={0} | all-to-all | bytes 1048576 | tf_op jit(solution)/shard_map/all_to_all | solution.py:133
  61.7 1.9 %collective-permute-start.3 = (bf16[2,512,256]{2,1,0:T(8,128)(2,1)S(1)}, bf16[2,512,256]{2,1,0:T(8,128)(2,1)S(1)}, u32[]{:S(2)}, u32[]{:S(2)}) collective-permute-start(bf16[2,512,256]{2,1,0:T(8,128)(2,1)S(1)} %given_0.1._), channel_id=1, source_target_pairs={{0,1},{1,0},{2,3},{3,2},{4,5},{5,4},{6,7},{7,6},{8,9},{9,8},{10,11... | collective-permute-start | bytes 1572872 | tf_op jit(solution)/shard_map/ppermute | solution.py:136
  63.6 0.5 given_1.1._
  64.1 2.4 %collective-permute-start.6 = (bf16[2,512,256]{2,1,0:T(8,128)(2,1)S(1)}, bf16[2,512,256]{2,1,0:T(8,128)(2,1)S(1)}, u32[]{:S(2)}, u32[]{:S(2)}) collective-permute-start(bf16[2,512,256]{2,1,0:T(8,128)(2,1)S(1)} %given_1.1._), channel_id=1, source_target_pairs={{0,1},{1,0},{2,3},{3,2},{4,5},{5,4},{6,7},{7,6},{8,9},{9,8},{10,11... | collective-permute-start | bytes 1572872 | tf_op jit(solution)/shard_map/ppermute | solution.py:136
  66.5 0.5 kept_0.1
  67.0 4.9 %collective-permute-start.4 = (bf16[512,256]{1,0:T(8,128)(2,1)S(1)}, bf16[512,256]{1,0:T(8,128)(2,1)S(1)}, u32[]{:S(2)}, u32[]{:S(2)}) collective-permute-start(bf16[512,256]{1,0:T(8,128)(2,1)S(1)} %across_0.1), channel_id=1, source_target_pairs={{0,2},{1,3},{2,0},{3,1},{4,6},{5,7},{6,4},{7,5},{8,10},{9,11},{10,... | collective-permute-start | bytes 786440 | tf_op jit(solution)/shard_map/ppermute | solution.py:136
  72.0 0.5 kept_1.1
  72.5 2.4 %collective-permute-start.7 = (bf16[512,256]{1,0:T(8,128)(2,1)S(1)}, bf16[512,256]{1,0:T(8,128)(2,1)S(1)}, u32[]{:S(2)}, u32[]{:S(2)}) collective-permute-start(bf16[512,256]{1,0:T(8,128)(2,1)S(1)} %across_1.1), channel_id=1, source_target_pairs={{0,2},{1,3},{2,0},{3,1},{4,6},{5,7},{6,4},{7,5},{8,10},{9,11},{10,... | collective-permute-start | bytes 786440 | tf_op jit(solution)/shard_map/ppermute | solution.py:136
  75.0 4.0 %collective-permute-done.4.crossed = bf16[512,256]{1,0:T(8,128)(2,1)S(1)} collective-permute-done((bf16[512,256]{1,0:T(8,128)(2,1)S(1)}, bf16[512,256]{1,0:T(8,128)(2,1)S(1)}, u32[]{:S(2)}, u32[]{:S(2)}) %collective-permute-start.4) | collective-permute-done | bytes 262176 | tf_op jit(solution)/shard_map/ppermute | solution.py:136
  79.1 14.8 %collective-permute-start.5 = (bf16[512,256]{1,0:T(8,128)(2,1)S(1)}, bf16[512,256]{1,0:T(8,128)(2,1)S(1)}, u32[]{:S(2)}, u32[]{:S(2)}) collective-permute-start(bf16[512,256]{1,0:T(8,128)(2,1)S(1)} %get-tuple-element.16), channel_id=1, source_target_pairs={{384,0},{400,16},{416,32},{432,48},{448,64},{464,80},{480,96},{496... | collective-permute-start | bytes 786440 | tf_op jit(solution)/shard_map/ppermute | solution.py:122
  94.1 5.1 %collective-permute-start.8 = (bf16[512,256]{1,0:T(8,128)(2,1)S(1)}, bf16[512,256]{1,0:T(8,128)(2,1)S(1)}, u32[]{:S(2)}, u32[]{:S(2)}) collective-permute-start(bf16[512,256]{1,0:T(8,128)(2,1)S(1)} %get-tuple-element.20), channel_id=1, source_target_pairs={{384,0},{400,16},{416,32},{432,48},{448,64},{464,80},{480,96},{496... | collective-permute-start | bytes 786440 | tf_op jit(solution)/shard_map/ppermute | solution.py:122
  99.2 36.0 %collective-permute-done.5.refs_1_ = bf16[512,256]{1,0:T(8,128)(2,1)S(1)} collective-permute-done((bf16[512,256]{1,0:T(8,128)(2,1)S(1)}, bf16[512,256]{1,0:T(8,128)(2,1)S(1)}, u32[]{:S(2)}, u32[]{:S(2)}) %collective-permute-start.5) | collective-permute-done | bytes 262176 | tf_op jit(solution)/shard_map/ppermute | solution.py:122
  135.3 4.6 %collective-permute-done.8.refs_3_ = bf16[512,256]{1,0:T(8,128)(2,1)S(1)} collective-permute-done((bf16[512,256]{1,0:T(8,128)(2,1)S(1)}, bf16[512,256]{1,0:T(8,128)(2,1)S(1)}, u32[]{:S(2)}, u32[]{:S(2)}) %collective-permute-start.8) | collective-permute-done | bytes 262176 | tf_op jit(solution)/shard_map/ppermute | solution.py:122
  139.8 1.1 average.1
  (27 shorter events, 1.4 us)
Async XLA Ops:
  0.0 1.6 %copy-start.4 = (bf16[1,128,8192]{2,1,0:T(8,128)(2,1)S(1)}, bf16[1,128,8192]{2,1,0:T(8,128)(2,1)}, u32[]{:S(2)}) copy-start(bf16[1,128,8192]{2,1,0:T(8,128)(2,1)} %param.4) | copy-start | bytes 6291460
  1.8 1.3 copy-start.1
  3.1 4.6 %copy-start = (f32[1,512,512]{2,1,0:T(8,128)S(1)}, f32[1,512,512]{2,1,0:T(8,128)}, u32[]{:S(2)}) copy-start(f32[1,512,512]{2,1,0:T(8,128)} %param.3) | copy-start | bytes 3145732
  3.1 30.9 %all-to-all-start = ((bf16[4,4,128,512]{3,2,1,0:T(8,128)(2,1)}), bf16[4,4,128,512]{3,2,1,0:T(8,128)(2,1)S(1)}, u32[]{:S(2)}, u32[]{:S(2)}) async-start(bf16[4,4,128,512]{3,2,1,0:T(8,128)(2,1)} %copy-done.1), calls=%async_computation | async-start | bytes 4194304 | tf_op jit(solution)/shard_map/all_to_all | solution.py:133
  7.7 42.9 %copy-start.11 = (bf16[1,128,512]{2,1,0:T(8,128)(2,1)S(1)}, bf16[1,128,512]{2,1,0:T(8,128)(2,1)}, u32[]{:S(2)}) copy-start(bf16[1,128,512]{2,1,0:T(8,128)(2,1)} %param.5) | copy-start | bytes 393220
  7.7 16.8 %collective-permute-start.1 = (bf16[512,512]{1,0:T(8,128)(2,1)S(1)}, bf16[512,512]{1,0:T(8,128)(2,1)S(1)}, u32[]{:S(2)}, u32[]{:S(2)}) collective-permute-start(bf16[512,512]{1,0:T(8,128)(2,1)S(1)} %round.1.refs_0_), channel_id=1, source_target_pairs={{0,2},{1,3},{2,0},{3,1},{4,6},{5,7},{6,4},{7,5},{8,10},{9,11},{10,... | collective-permute-start | bytes 1572872 | tf_op jit(solution)/shard_map/ppermute | solution.py:136
  12.7 14.6 %collective-permute-start = (bf16[512,512]{1,0:T(8,128)(2,1)S(1)}, bf16[512,512]{1,0:T(8,128)(2,1)S(1)}, u32[]{:S(2)}, u32[]{:S(2)}) collective-permute-start(bf16[512,512]{1,0:T(8,128)(2,1)S(1)} %round.1.refs_0_), channel_id=1, source_target_pairs={{0,1},{1,0},{2,3},{3,2},{4,5},{5,4},{6,7},{7,6},{8,9},{9,8},{10,11... | collective-permute-start | bytes 1572872 | tf_op jit(solution)/shard_map/ppermute | solution.py:136
  14.6 0.8 copy-start.2
  24.5 3.8 %collective-permute-start.2 = (bf16[512,512]{1,0:T(8,128)(2,1)S(1)}, bf16[512,512]{1,0:T(8,128)(2,1)S(1)}, u32[]{:S(2)}, u32[]{:S(2)}) collective-permute-start(bf16[512,512]{1,0:T(8,128)(2,1)S(1)} %collective-permute-done.1.refs_2_), channel_id=1, source_target_pairs={{0,1},{1,0},{2,3},{3,2},{4,5},{5,4},{6,7},{7,6},{8,9},{9,8},{10,11... | collective-permute-start | bytes 1572872 | tf_op jit(solution)/shard_map/ppermute | solution.py:136
  26.4 0.8 copy-start.5
  27.2 0.8 copy-start.7
  28.3 0.8 copy-start.9
  34.0 1.0 copy-start.3
  35.1 1.0 copy-start.6
  36.1 1.0 copy-start.8
  37.1 1.0 copy-start.10
  61.7 5.3 %collective-permute-start.3 = (bf16[2,512,256]{2,1,0:T(8,128)(2,1)S(1)}, bf16[2,512,256]{2,1,0:T(8,128)(2,1)S(1)}, u32[]{:S(2)}, u32[]{:S(2)}) collective-permute-start(bf16[2,512,256]{2,1,0:T(8,128)(2,1)S(1)} %given_0.1._), channel_id=1, source_target_pairs={{0,1},{1,0},{2,3},{3,2},{4,5},{5,4},{6,7},{7,6},{8,9},{9,8},{10,11... | collective-permute-start | bytes 1572872 | tf_op jit(solution)/shard_map/ppermute | solution.py:136
  64.1 8.4 %collective-permute-start.6 = (bf16[2,512,256]{2,1,0:T(8,128)(2,1)S(1)}, bf16[2,512,256]{2,1,0:T(8,128)(2,1)S(1)}, u32[]{:S(2)}, u32[]{:S(2)}) collective-permute-start(bf16[2,512,256]{2,1,0:T(8,128)(2,1)S(1)} %given_1.1._), channel_id=1, source_target_pairs={{0,1},{1,0},{2,3},{3,2},{4,5},{5,4},{6,7},{7,6},{8,9},{9,8},{10,11... | collective-permute-start | bytes 1572872 | tf_op jit(solution)/shard_map/ppermute | solution.py:136
  67.0 12.0 %collective-permute-start.4 = (bf16[512,256]{1,0:T(8,128)(2,1)S(1)}, bf16[512,256]{1,0:T(8,128)(2,1)S(1)}, u32[]{:S(2)}, u32[]{:S(2)}) collective-permute-start(bf16[512,256]{1,0:T(8,128)(2,1)S(1)} %across_0.1), channel_id=1, source_target_pairs={{0,2},{1,3},{2,0},{3,1},{4,6},{5,7},{6,4},{7,5},{8,10},{9,11},{10,... | collective-permute-start | bytes 786440 | tf_op jit(solution)/shard_map/ppermute | solution.py:136
  72.5 21.4 %collective-permute-start.7 = (bf16[512,256]{1,0:T(8,128)(2,1)S(1)}, bf16[512,256]{1,0:T(8,128)(2,1)S(1)}, u32[]{:S(2)}, u32[]{:S(2)}) collective-permute-start(bf16[512,256]{1,0:T(8,128)(2,1)S(1)} %across_1.1), channel_id=1, source_target_pairs={{0,2},{1,3},{2,0},{3,1},{4,6},{5,7},{6,4},{7,5},{8,10},{9,11},{10,... | collective-permute-start | bytes 786440 | tf_op jit(solution)/shard_map/ppermute | solution.py:136
  79.1 56.1 %collective-permute-start.5 = (bf16[512,256]{1,0:T(8,128)(2,1)S(1)}, bf16[512,256]{1,0:T(8,128)(2,1)S(1)}, u32[]{:S(2)}, u32[]{:S(2)}) collective-permute-start(bf16[512,256]{1,0:T(8,128)(2,1)S(1)} %get-tuple-element.16), channel_id=1, source_target_pairs={{384,0},{400,16},{416,32},{432,48},{448,64},{464,80},{480,96},{496... | collective-permute-start | bytes 786440 | tf_op jit(solution)/shard_map/ppermute | solution.py:122
  94.1 45.7 %collective-permute-start.8 = (bf16[512,256]{1,0:T(8,128)(2,1)S(1)}, bf16[512,256]{1,0:T(8,128)(2,1)S(1)}, u32[]{:S(2)}, u32[]{:S(2)}) collective-permute-start(bf16[512,256]{1,0:T(8,128)(2,1)S(1)} %get-tuple-element.20), channel_id=1, source_target_pairs={{384,0},{400,16},{416,32},{432,48},{448,64},{464,80},{480,96},{496... | collective-permute-start | bytes 786440 | tf_op jit(solution)/shard_map/ppermute | solution.py:122

commit v4 on v3

--- a/solution.py
+++ b/solution.py
@@ -19,14 +19,13 @@
 BF16 = jnp.bfloat16
 
 
-def call(kernel, name, outs, ins, scratch=()):
+def call(kernel, name, outs, ins):
     return pl.pallas_call(
         kernel,
         name=name,
         out_shape=[jax.ShapeDtypeStruct(s, d) for s, d in outs],
         in_specs=list(ins),
         out_specs=[VMEM] * len(outs),
-        scratch_shapes=list(scratch),
         compiler_params=pltpu.CompilerParams(vmem_limit_bytes=8 * 1024 * 1024),
         cost_estimate=pl.CostEstimate(flops=1_000_000, bytes_accessed=1_000_000, transcendentals=0),
     )
@@ -45,16 +44,14 @@
             blocks[y, k] = features[:, pl.ds(start, rows)]
 
 
-def keys_kernel(blocks, *refs):
-    *sources, out, working, sem = refs
+def stack_kernel(*refs):
+    *sources, out = refs
+    for k, source in enumerate(sources):
+        out[k] = source[...]
+
+
+def keys_kernel(blocks, working, out):
     ring, _, count, rows = blocks.shape
-    copies = [
-        pltpu.make_async_copy(source, working.at[k], sem.at[k]) for k, source in enumerate(sources)
-    ]
-    for copy in copies:
-        copy.start()
-    for copy in copies:
-        copy.wait()
     for c in range(0, out.shape[2], 256):
         part = slice(c, c + 256)
         total = sum(
@@ -144,19 +141,15 @@
     (working,) = call(round_kernel, "round", [((rows, width), BF16)], [VMEM])(master)
     beside = swap(working, 1)
     across = swap(working, 2)
-    working = [working, beside, across, swap(across, 1)]
+    (working,) = call(stack_kernel, "stack", [((SIDE, rows, width), BF16)], [VMEM] * SIDE)(
+        working, beside, across, swap(across, 1)
+    )
     shape = (ring, SIDE, count, rows)
     (blocks,) = call(block_kernel, "block", [(shape, BF16)], [VMEM])(tokens)
     blocks = exchange(blocks)
 
     shape = (ring, count, width)
-    (partial,) = call(
-        keys_kernel,
-        "keys",
-        [(shape, BF16)],
-        [VMEM] + [ANY] * SIDE,
-        scratch=[pltpu.VMEM((SIDE, rows, width), BF16), pltpu.SemaphoreType.DMA((SIDE,))],
-    )(blocks, *working)
+    (partial,) = call(keys_kernel, "keys", [(shape, BF16)], [VMEM] * 2)(blocks, working)
     (error,) = call(error_kernel, "error", [(shape, BF16)], [VMEM] * 2)(exchange(partial), targets)
     errors = exchange(error)
 

time: 142 us -> 139 us (0.979)
  local copies, waits for them, and re-layouts: 10.3 us -> 5.82 us
  waiting for transfers between devices: 58.9 us -> 60.7 us
    unnamed x24 -> x12, local copies, waits for them, and re-layouts: 10.3 us -> 5.82 us
    ppermute x7, waiting for transfers between devices: 13.4 us -> 15.8 us  [swap(): return lax.ppermute(block, 'fsdp', [(i, i ^ k) for i in range(size)])]
where the time goes in v4:
time: 139 us; the launch traced here: 138 us
  waiting for transfers between devices  60.7 us (44%)
  starting transfers between devices  45 us (32%)
  blocking collectives  21.4 us (15%)
  local copies, waits for them, and re-layouts  5.82 us (4%)
  Pallas kernels  5.03 us (4%)
    ppermute x2, waiting for transfers between devices, from_behind(): return lax.ppermute(block, axis, route)  40.6 us
    all_to_all x2, blocking collectives, exchange(): return lax.all_to_all(blocks, 'fsdp', 0, 0, axis_index_groups=groups)  21.4 us
    ppermute x7, starting transfers between devices, swap(): return lax.ppermute(block, 'fsdp', [(i, i ^ k) for i in range(size)])  20.4 us
    ppermute x2, starting transfers between devices, from_behind(): return lax.ppermute(block, axis, route)  20 us
    ppermute x7, waiting for transfers between devices, swap(): return lax.ppermute(block, 'fsdp', [(i, i ^ k) for i in range(size)])  15.8 us
    unnamed x12, local copies, waits for them, and re-layouts  5.82 us
    all_to_all x1, starting transfers between devices, exchange(): return lax.all_to_all(blocks, 'fsdp', 0, 0, axis_index_groups=groups)  4.59 us
    all_to_all x1, waiting for transfers between devices, exchange(): return lax.all_to_all(blocks, 'fsdp', 0, 0, axis_index_groups=groups)  4.24 us
  transfers between devices with their start and end apart: 10, of which 6 were waited for; matrix products, arithmetic and copies ran while one was open for 0% of the time, Pallas kernels for 1%

profile of v4, /device:TPU:32, one launch (start us, length us, event | category | flops | bytes accessed | tf_op | source)
XLA Modules:
  0.0 138.2 jit_solution(637974516514743527)
XLA Ops:
  0.0 1.6 %copy-done.4 = bf16[1,128,8192]{2,1,0:T(8,128)(2,1)S(1)} copy-done((bf16[1,128,8192]{2,1,0:T(8,128)(2,1)S(1)}, bf16[1,128,8192]{2,1,0:T(8,128)(2,1)}, u32[]{:S(2)}) %copy-start.4) | copy-done | bytes 2097176
  1.6 0.2 block.1
  1.8 1.3 copy-done.1
  3.1 4.6 %all-to-all-start = ((bf16[4,4,128,512]{3,2,1,0:T(8,128)(2,1)}), bf16[4,4,128,512]{3,2,1,0:T(8,128)(2,1)S(1)}, u32[]{:S(2)}, u32[]{:S(2)}) async-start(bf16[4,4,128,512]{3,2,1,0:T(8,128)(2,1)} %copy-done.1), calls=%async_computation | async-start | bytes 4194304 | tf_op jit(solution)/shard_map/all_to_all | solution.py:130
  7.8 4.9 %collective-permute-start.1 = (bf16[512,512]{1,0:T(8,128)(2,1)S(1)}, bf16[512,512]{1,0:T(8,128)(2,1)S(1)}, u32[]{:S(2)}, u32[]{:S(2)}) collective-permute-start(bf16[512,512]{1,0:T(8,128)(2,1)S(1)} %round.1.refs_0_), channel_id=1, source_target_pairs={{0,2},{1,3},{2,0},{3,1},{4,6},{5,7},{6,4},{7,5},{8,10},{9,11},{10,... | collective-permute-start | bytes 1572872 | tf_op jit(solution)/shard_map/ppermute | solution.py:133
  12.7 1.9 %collective-permute-start = (bf16[512,512]{1,0:T(8,128)(2,1)S(1)}, bf16[512,512]{1,0:T(8,128)(2,1)S(1)}, u32[]{:S(2)}, u32[]{:S(2)}) collective-permute-start(bf16[512,512]{1,0:T(8,128)(2,1)S(1)} %round.1.refs_0_), channel_id=1, source_target_pairs={{0,1},{1,0},{2,3},{3,2},{4,5},{5,4},{6,7},{7,6},{8,9},{9,8},{10,11... | collective-permute-start | bytes 1572872 | tf_op jit(solution)/shard_map/ppermute | solution.py:133
  14.6 9.9 %collective-permute-done.1.refs_2_ = bf16[512,512]{1,0:T(8,128)(2,1)S(1)} collective-permute-done((bf16[512,512]{1,0:T(8,128)(2,1)S(1)}, bf16[512,512]{1,0:T(8,128)(2,1)S(1)}, u32[]{:S(2)}, u32[]{:S(2)}) %collective-permute-start.1) | collective-permute-done | bytes 524320 | tf_op jit(solution)/shard_map/ppermute | solution.py:133
  24.5 1.9 %collective-permute-start.2 = (bf16[512,512]{1,0:T(8,128)(2,1)S(1)}, bf16[512,512]{1,0:T(8,128)(2,1)S(1)}, u32[]{:S(2)}, u32[]{:S(2)}) collective-permute-start(bf16[512,512]{1,0:T(8,128)(2,1)S(1)} %collective-permute-done.1.refs_2_), channel_id=1, source_target_pairs={{0,1},{1,0},{2,3},{3,2},{4,5},{5,4},{6,7},{7,6},{8,9},{9,8},{10,11... | collective-permute-start | bytes 1572872 | tf_op jit(solution)/shard_map/ppermute | solution.py:133
  26.5 1.9 %collective-permute-done.2.refs_3_ = bf16[512,512]{1,0:T(8,128)(2,1)S(1)} collective-permute-done((bf16[512,512]{1,0:T(8,128)(2,1)S(1)}, bf16[512,512]{1,0:T(8,128)(2,1)S(1)}, u32[]{:S(2)}, u32[]{:S(2)}) %collective-permute-start.2) | collective-permute-done | bytes 524320 | tf_op jit(solution)/shard_map/ppermute | solution.py:133
  28.3 0.1 stack.1.working
  28.5 1.3 copy-done.2
  29.8 4.2 %all-to-all-done.blocks = bf16[4,4,128,512]{3,2,1,0:T(8,128)(2,1)S(1)} async-done(((bf16[4,4,128,512]{3,2,1,0:T(8,128)(2,1)}), bf16[4,4,128,512]{3,2,1,0:T(8,128)(2,1)S(1)}, u32[]{:S(2)}, u32[]{:S(2)}) %all-to-all-start) | async-done | bytes 2097184 | tf_op jit(solution)/shard_map/all_to_all | solution.py:130
  34.0 1.6 %copy-done.3 = bf16[4,512,512]{2,1,0:T(8,128)(2,1)S(1)} copy-done((bf16[4,512,512]{2,1,0:T(8,128)(2,1)S(1)}, bf16[4,512,512]{2,1,0:T(8,128)(2,1)}, u32[]{:S(2)}) %copy-start.3) | copy-done | bytes 2097176
  35.6 1.2 keys.1
  36.9 11.0 %all_to_all.15.parts = bf16[4,128,512]{2,1,0:T(8,128)(2,1)S(1)} all-to-all(bf16[4,128,512]{2,1,0:T(8,128)(2,1)S(1)} %keys.1), channel_id=1, replica_groups={{0,4,8,12},{1,5,9,13},{2,6,10,14},{3,7,11,15},{16,20,24,28},{17,21,25,2..., dimensions={0} | all-to-all | bytes 1048576 | tf_op jit(solution)/shard_map/all_to_all | solution.py:130
  47.9 10.5 %all_to_all.16.errors = bf16[4,128,512]{2,1,0:T(8,128)(2,1)S(1)} all-to-all(bf16[4,128,512]{2,1,0:T(8,128)(2,1)S(1)} %error.1), channel_id=1, replica_groups={{0,4,8,12},{1,5,9,13},{2,6,10,14},{3,7,11,15},{16,20,24,28},{17,21,25,2..., dimensions={0} | all-to-all | bytes 1048576 | tf_op jit(solution)/shard_map/all_to_all | solution.py:130
  58.4 0.5 given_0.1._
  58.9 1.9 %collective-permute-start.3 = (bf16[2,512,256]{2,1,0:T(8,128)(2,1)S(1)}, bf16[2,512,256]{2,1,0:T(8,128)(2,1)S(1)}, u32[]{:S(2)}, u32[]{:S(2)}) collective-permute-start(bf16[2,512,256]{2,1,0:T(8,128)(2,1)S(1)} %given_0.1._), channel_id=1, source_target_pairs={{0,1},{1,0},{2,3},{3,2},{4,5},{5,4},{6,7},{7,6},{8,9},{9,8},{10,11... | collective-permute-start | bytes 1572872 | tf_op jit(solution)/shard_map/ppermute | solution.py:133
  60.8 0.5 given_1.1._
  61.3 2.4 %collective-permute-start.6 = (bf16[2,512,256]{2,1,0:T(8,128)(2,1)S(1)}, bf16[2,512,256]{2,1,0:T(8,128)(2,1)S(1)}, u32[]{:S(2)}, u32[]{:S(2)}) collective-permute-start(bf16[2,512,256]{2,1,0:T(8,128)(2,1)S(1)} %given_1.1._), channel_id=1, source_target_pairs={{0,1},{1,0},{2,3},{3,2},{4,5},{5,4},{6,7},{7,6},{8,9},{9,8},{10,11... | collective-permute-start | bytes 1572872 | tf_op jit(solution)/shard_map/ppermute | solution.py:133
  63.7 0.5 kept_0.1
  64.3 4.9 %collective-permute-start.4 = (bf16[512,256]{1,0:T(8,128)(2,1)S(1)}, bf16[512,256]{1,0:T(8,128)(2,1)S(1)}, u32[]{:S(2)}, u32[]{:S(2)}) collective-permute-start(bf16[512,256]{1,0:T(8,128)(2,1)S(1)} %across_0.1), channel_id=1, source_target_pairs={{0,2},{1,3},{2,0},{3,1},{4,6},{5,7},{6,4},{7,5},{8,10},{9,11},{10,... | collective-permute-start | bytes 786440 | tf_op jit(solution)/shard_map/ppermute | solution.py:133
  69.2 0.5 kept_1.1
  69.8 2.4 %collective-permute-start.7 = (bf16[512,256]{1,0:T(8,128)(2,1)S(1)}, bf16[512,256]{1,0:T(8,128)(2,1)S(1)}, u32[]{:S(2)}, u32[]{:S(2)}) collective-permute-start(bf16[512,256]{1,0:T(8,128)(2,1)S(1)} %across_1.1), channel_id=1, source_target_pairs={{0,2},{1,3},{2,0},{3,1},{4,6},{5,7},{6,4},{7,5},{8,10},{9,11},{10,... | collective-permute-start | bytes 786440 | tf_op jit(solution)/shard_map/ppermute | solution.py:133
  72.2 4.0 %collective-permute-done.4.crossed = bf16[512,256]{1,0:T(8,128)(2,1)S(1)} collective-permute-done((bf16[512,256]{1,0:T(8,128)(2,1)S(1)}, bf16[512,256]{1,0:T(8,128)(2,1)S(1)}, u32[]{:S(2)}, u32[]{:S(2)}) %collective-permute-start.4) | collective-permute-done | bytes 262176 | tf_op jit(solution)/shard_map/ppermute | solution.py:133
  76.3 0.1 step_0.1
  76.4 14.8 %collective-permute-start.5 = (bf16[512,256]{1,0:T(8,128)(2,1)S(1)}, bf16[512,256]{1,0:T(8,128)(2,1)S(1)}, u32[]{:S(2)}, u32[]{:S(2)}) collective-permute-start(bf16[512,256]{1,0:T(8,128)(2,1)S(1)} %get-tuple-element.16), channel_id=1, source_target_pairs={{384,0},{400,16},{416,32},{432,48},{448,64},{464,80},{480,96},{496... | collective-permute-start | bytes 786440 | tf_op jit(solution)/shard_map/ppermute | solution.py:119
  91.2 0.1 step_1.1
  91.4 5.1 %collective-permute-start.8 = (bf16[512,256]{1,0:T(8,128)(2,1)S(1)}, bf16[512,256]{1,0:T(8,128)(2,1)S(1)}, u32[]{:S(2)}, u32[]{:S(2)}) collective-permute-start(bf16[512,256]{1,0:T(8,128)(2,1)S(1)} %get-tuple-element.20), channel_id=1, source_target_pairs={{384,0},{400,16},{416,32},{432,48},{448,64},{464,80},{480,96},{496... | collective-permute-start | bytes 786440 | tf_op jit(solution)/shard_map/ppermute | solution.py:119
  96.5 36.0 %collective-permute-done.5.refs_1_ = bf16[512,256]{1,0:T(8,128)(2,1)S(1)} collective-permute-done((bf16[512,256]{1,0:T(8,128)(2,1)S(1)}, bf16[512,256]{1,0:T(8,128)(2,1)S(1)}, u32[]{:S(2)}, u32[]{:S(2)}) %collective-permute-start.5) | collective-permute-done | bytes 262176 | tf_op jit(solution)/shard_map/ppermute | solution.py:119
  132.5 4.6 %collective-permute-done.8.refs_3_ = bf16[512,256]{1,0:T(8,128)(2,1)S(1)} collective-permute-done((bf16[512,256]{1,0:T(8,128)(2,1)S(1)}, bf16[512,256]{1,0:T(8,128)(2,1)S(1)}, u32[]{:S(2)}, u32[]{:S(2)}) %collective-permute-start.8) | collective-permute-done | bytes 262176 | tf_op jit(solution)/shard_map/ppermute | solution.py:119
  137.1 1.1 average.1
  (16 shorter events, 0.3 us)
Async XLA Ops:
  0.0 1.6 %copy-start.4 = (bf16[1,128,8192]{2,1,0:T(8,128)(2,1)S(1)}, bf16[1,128,8192]{2,1,0:T(8,128)(2,1)}, u32[]{:S(2)}) copy-start(bf16[1,128,8192]{2,1,0:T(8,128)(2,1)} %param.4) | copy-start | bytes 6291460
  1.8 1.3 copy-start.1
  3.1 4.6 %copy-start = (f32[1,512,512]{2,1,0:T(8,128)S(1)}, f32[1,512,512]{2,1,0:T(8,128)}, u32[]{:S(2)}) copy-start(f32[1,512,512]{2,1,0:T(8,128)} %param.3) | copy-start | bytes 3145732
  3.1 30.9 %all-to-all-start = ((bf16[4,4,128,512]{3,2,1,0:T(8,128)(2,1)}), bf16[4,4,128,512]{3,2,1,0:T(8,128)(2,1)S(1)}, u32[]{:S(2)}, u32[]{:S(2)}) async-start(bf16[4,4,128,512]{3,2,1,0:T(8,128)(2,1)} %copy-done.1), calls=%async_computation | async-start | bytes 4194304 | tf_op jit(solution)/shard_map/all_to_all | solution.py:130
  7.8 16.8 %collective-permute-start.1 = (bf16[512,512]{1,0:T(8,128)(2,1)S(1)}, bf16[512,512]{1,0:T(8,128)(2,1)S(1)}, u32[]{:S(2)}, u32[]{:S(2)}) collective-permute-start(bf16[512,512]{1,0:T(8,128)(2,1)S(1)} %round.1.refs_0_), channel_id=1, source_target_pairs={{0,2},{1,3},{2,0},{3,1},{4,6},{5,7},{6,4},{7,5},{8,10},{9,11},{10,... | collective-permute-start | bytes 1572872 | tf_op jit(solution)/shard_map/ppermute | solution.py:133
  12.7 13.8 %collective-permute-start = (bf16[512,512]{1,0:T(8,128)(2,1)S(1)}, bf16[512,512]{1,0:T(8,128)(2,1)S(1)}, u32[]{:S(2)}, u32[]{:S(2)}) collective-permute-start(bf16[512,512]{1,0:T(8,128)(2,1)S(1)} %round.1.refs_0_), channel_id=1, source_target_pairs={{0,1},{1,0},{2,3},{3,2},{4,5},{5,4},{6,7},{7,6},{8,9},{9,8},{10,11... | collective-permute-start | bytes 1572872 | tf_op jit(solution)/shard_map/ppermute | solution.py:133
  24.5 3.8 %collective-permute-start.2 = (bf16[512,512]{1,0:T(8,128)(2,1)S(1)}, bf16[512,512]{1,0:T(8,128)(2,1)S(1)}, u32[]{:S(2)}, u32[]{:S(2)}) collective-permute-start(bf16[512,512]{1,0:T(8,128)(2,1)S(1)} %collective-permute-done.1.refs_2_), channel_id=1, source_target_pairs={{0,1},{1,0},{2,3},{3,2},{4,5},{5,4},{6,7},{7,6},{8,9},{9,8},{10,11... | collective-permute-start | bytes 1572872 | tf_op jit(solution)/shard_map/ppermute | solution.py:133
  28.5 1.3 copy-start.2
  34.0 1.6 %copy-start.3 = (bf16[4,512,512]{2,1,0:T(8,128)(2,1)S(1)}, bf16[4,512,512]{2,1,0:T(8,128)(2,1)}, u32[]{:S(2)}) copy-start(bf16[4,512,512]{2,1,0:T(8,128)(2,1)} %copy-done.2) | copy-start | bytes 6291460
  35.6 12.2 %copy-start.5 = (bf16[1,128,512]{2,1,0:T(8,128)(2,1)S(1)}, bf16[1,128,512]{2,1,0:T(8,128)(2,1)}, u32[]{:S(2)}) copy-start(bf16[1,128,512]{2,1,0:T(8,128)(2,1)} %param.5) | copy-start | bytes 393220
  58.9 5.3 %collective-permute-start.3 = (bf16[2,512,256]{2,1,0:T(8,128)(2,1)S(1)}, bf16[2,512,256]{2,1,0:T(8,128)(2,1)S(1)}, u32[]{:S(2)}, u32[]{:S(2)}) collective-permute-start(bf16[2,512,256]{2,1,0:T(8,128)(2,1)S(1)} %given_0.1._), channel_id=1, source_target_pairs={{0,1},{1,0},{2,3},{3,2},{4,5},{5,4},{6,7},{7,6},{8,9},{9,8},{10,11... | collective-permute-start | bytes 1572872 | tf_op jit(solution)/shard_map/ppermute | solution.py:133
  61.3 8.4 %collective-permute-start.6 = (bf16[2,512,256]{2,1,0:T(8,128)(2,1)S(1)}, bf16[2,512,256]{2,1,0:T(8,128)(2,1)S(1)}, u32[]{:S(2)}, u32[]{:S(2)}) collective-permute-start(bf16[2,512,256]{2,1,0:T(8,128)(2,1)S(1)} %given_1.1._), channel_id=1, source_target_pairs={{0,1},{1,0},{2,3},{3,2},{4,5},{5,4},{6,7},{7,6},{8,9},{9,8},{10,11... | collective-permute-start | bytes 1572872 | tf_op jit(solution)/shard_map/ppermute | solution.py:133
  64.3 12.0 %collective-permute-start.4 = (bf16[512,256]{1,0:T(8,128)(2,1)S(1)}, bf16[512,256]{1,0:T(8,128)(2,1)S(1)}, u32[]{:S(2)}, u32[]{:S(2)}) collective-permute-start(bf16[512,256]{1,0:T(8,128)(2,1)S(1)} %across_0.1), channel_id=1, source_target_pairs={{0,2},{1,3},{2,0},{3,1},{4,6},{5,7},{6,4},{7,5},{8,10},{9,11},{10,... | collective-permute-start | bytes 786440 | tf_op jit(solution)/shard_map/ppermute | solution.py:133
  69.8 21.4 %collective-permute-start.7 = (bf16[512,256]{1,0:T(8,128)(2,1)S(1)}, bf16[512,256]{1,0:T(8,128)(2,1)S(1)}, u32[]{:S(2)}, u32[]{:S(2)}) collective-permute-start(bf16[512,256]{1,0:T(8,128)(2,1)S(1)} %across_1.1), channel_id=1, source_target_pairs={{0,2},{1,3},{2,0},{3,1},{4,6},{5,7},{6,4},{7,5},{8,10},{9,11},{10,... | collective-permute-start | bytes 786440 | tf_op jit(solution)/shard_map/ppermute | solution.py:133
  76.4 56.1 %collective-permute-start.5 = (bf16[512,256]{1,0:T(8,128)(2,1)S(1)}, bf16[512,256]{1,0:T(8,128)(2,1)S(1)}, u32[]{:S(2)}, u32[]{:S(2)}) collective-permute-start(bf16[512,256]{1,0:T(8,128)(2,1)S(1)} %get-tuple-element.16), channel_id=1, source_target_pairs={{384,0},{400,16},{416,32},{432,48},{448,64},{464,80},{480,96},{496... | collective-permute-start | bytes 786440 | tf_op jit(solution)/shard_map/ppermute | solution.py:119
  91.4 45.7 %collective-permute-start.8 = (bf16[512,256]{1,0:T(8,128)(2,1)S(1)}, bf16[512,256]{1,0:T(8,128)(2,1)S(1)}, u32[]{:S(2)}, u32[]{:S(2)}) collective-permute-start(bf16[512,256]{1,0:T(8,128)(2,1)S(1)} %get-tuple-element.20), channel_id=1, source_target_pairs={{384,0},{400,16},{416,32},{432,48},{448,64},{464,80},{480,96},{496... | collective-permute-start | bytes 786440 | tf_op jit(solution)/shard_map/ppermute | solution.py:119

commit v5 on v4

--- a/solution.py
+++ b/solution.py
@@ -10,6 +10,8 @@
 D = 8192
 STEP = 3
 PIECES = (256, 256)
+FLOPS = 10_000_000_000
+KEPT = (1_000_000, 10_000_000_000)
 SIDE = 4
 SCALE = 1.0 / D**0.5
 
@@ -19,7 +21,7 @@
 BF16 = jnp.bfloat16
 
 
-def call(kernel, name, outs, ins):
+def call(kernel, name, outs, ins, flops=1_000_000):
     return pl.pallas_call(
         kernel,
         name=name,
@@ -27,7 +29,7 @@
         in_specs=list(ins),
         out_specs=[VMEM] * len(outs),
         compiler_params=pltpu.CompilerParams(vmem_limit_bytes=8 * 1024 * 1024),
-        cost_estimate=pl.CostEstimate(flops=1_000_000, bytes_accessed=1_000_000, transcendentals=0),
+        cost_estimate=pl.CostEstimate(flops=flops, bytes_accessed=1_000_000, transcendentals=0),
     )
 
 
@@ -35,13 +37,22 @@
     working[...] = master[...].astype(BF16)
 
 
-def block_kernel(features, blocks):
+def block_kernel(features, blocks, held, sem):
     mine = lax.rem(lax.axis_index("fsdp"), SIDE)
     ring, _, _, rows = blocks.shape
-    for k in range(SIDE):
-        for y in range(ring):
-            start = pl.multiple_of((y * SIDE + (mine ^ k)) * rows, rows)
-            blocks[y, k] = features[:, pl.ds(start, rows)]
+    places = [(y, k) for y in range(ring) for k in range(SIDE)]
+    reads, writes = [], []
+    for y, k in places:
+        start = pl.multiple_of((y * SIDE + (mine ^ k)) * rows, rows)
+        source = features.at[:, pl.ds(start, rows)]
+        reads.append(pltpu.make_async_copy(source, held.at[y, k], sem.at[0, y, k]))
+        writes.append(pltpu.make_async_copy(held.at[y, k], blocks.at[y, k], sem.at[1, y, k]))
+        reads[-1].start()
+    for read, write in zip(reads, writes):
+        read.wait()
+        write.start()
+    for write in writes:
+        write.wait()
 
 
 def stack_kernel(*refs):
@@ -86,7 +97,8 @@
     )
 
 
-def given_kernel(start, stop, blocks, errors, out):
+def given_kernel(start, stop, blocks, errors, *rest):
+    out = rest[-1]
     for i, k in enumerate((3, 1)):
         out[i] = term(blocks, errors, k, start, stop).astype(BF16)
 
@@ -107,10 +119,18 @@
     sent[...] = new.astype(BF16)
 
 
-def average_kernel(chunks, *refs):
-    out = refs[-1]
-    for i, (start, stop) in enumerate(chunks):
-        out[:, start:stop] = 0.5 * (refs[2 * i][...] + refs[2 * i + 1][...].astype(F32))
+def mean_kernel(stepped, other, out):
+    out[...] = 0.5 * (stepped[...] + other[...].astype(F32))
+
+
+def average_kernel(*refs):
+    *means, stepped, other, out = refs
+    start = 0
+    for mean in means:
+        stop = start + mean.shape[1]
+        out[:, start:stop] = mean[...]
+        start = stop
+    out[:, start:] = 0.5 * (stepped[...] + other[...].astype(F32))
 
 
 def from_behind(block, axis, distance):
@@ -145,7 +165,15 @@
         working, beside, across, swap(across, 1)
     )
     shape = (ring, SIDE, count, rows)
-    (blocks,) = call(block_kernel, "block", [(shape, BF16)], [VMEM])(tokens)
+    blocks = pl.pallas_call(
+        block_kernel,
+        name="block",
+        out_shape=jax.ShapeDtypeStruct(shape, BF16),
+        in_specs=[pl.BlockSpec(memory_space=pl.ANY)],
+        out_specs=pl.BlockSpec(memory_space=pl.ANY),
+        scratch_shapes=[pltpu.VMEM(shape, BF16), pltpu.SemaphoreType.DMA((2, ring, SIDE))],
+        compiler_params=pltpu.CompilerParams(vmem_limit_bytes=60 * 1024 * 1024),
+    )(tokens)
     blocks = exchange(blocks)
 
     shape = (ring, count, width)
@@ -153,36 +181,43 @@
     (error,) = call(error_kernel, "error", [(shape, BF16)], [VMEM] * 2)(exchange(partial), targets)
     errors = exchange(error)
 
-    results = []
+    results, after = [], []
     for h, (start, stop) in enumerate(chunks):
         half = (rows, stop - start)
+        weight = max((len(chunks) - 1 - h) * FLOPS, 1_000_000)
+        mean_weight = weight if len(chunks) == 2 else 1_000_000
         (given,) = call(
             functools.partial(given_kernel, start, stop),
             f"given_{h}",
             [((2, *half), BF16)],
-            [VMEM] * 2,
-        )(blocks, errors)
+            [VMEM] * 2 + [ANY] * len(after),
+        )(blocks, errors, *after)
         across, kept = call(
             functools.partial(kept_kernel, start, stop),
             f"kept_{h}",
             [(half, F32)] * 2,
             [VMEM] * 2 + [ANY],
+            KEPT[h],
         )(blocks, errors, given)
         given = swap(given, 1)
-        (across,) = call(across_kernel, f"across_{h}", [(half, BF16)], [VMEM] * 2)(across, given)
+        (across,) = call(across_kernel, f"across_{h}", [(half, BF16)], [VMEM] * 2, weight)(
+            across, given
+        )
+        after = [across]
         stepped, sent = call(
             functools.partial(step_kernel, start, stop),
             f"step_{h}",
             [(half, F32), (half, BF16)],
             [VMEM] * 4,
+            weight,
         )(kept, given, swap(across, 2), master)
-        results += [stepped, from_behind(sent, "rep", hop)]
-    (updated,) = call(
-        functools.partial(average_kernel, chunks),
-        "average",
-        [((rows, width), F32)],
-        [VMEM] * len(results),
-    )(*results)
+        result = (stepped, from_behind(sent, "rep", hop))
+        if h < len(chunks) - 1:
+            result = call(mean_kernel, f"mean_{h}", [(half, F32)], [VMEM] * 2, mean_weight)(*result)
+        results += result
+    (updated,) = call(average_kernel, "average", [((rows, width), F32)], [VMEM] * len(results))(
+        *results
+    )
     return updated[None]
 
 

time: 139 us -> 138 us (level)
  waiting for transfers between devices: 60.7 us -> 56.4 us
  starting transfers between devices: 45 us -> 48.5 us
  local copies, waits for them, and re-layouts: 5.82 us -> 2.91 us
  Pallas kernels: 5.03 us -> 7.55 us
    ppermute x2, starting transfers between devices: 20 us -> 24 us  [from_behind(): return lax.ppermute(block, axis, route)]
    ppermute x2, waiting for transfers between devices: 40.6 us -> 37.6 us  [from_behind(): return lax.ppermute(block, axis, route)]
    unnamed x12 -> x8, local copies, waits for them, and re-layouts: 5.82 us -> 2.91 us
    pallas_call x4 -> x5, Pallas kernels: 1.32 us -> 3.84 us  [the longest x1 2.63 us: body(): pl.pallas_call(block_kernel, name='block', out_shape=jax.ShapeDtypeStruct...]
  transfers between devices with their start and end apart: 10 -> 10, of which waited for: 6 -> 7; matrix products, arithmetic and copies ran while one was open for 0% -> 0% of each run, Pallas kernels for 1% -> 1%
where the time goes in v5:
time: 138 us; the launch traced here: 137 us
  waiting for transfers between devices  56.4 us (41%)
  starting transfers between devices  48.5 us (35%)
  blocking collectives  21.4 us (16%)
  Pallas kernels  7.55 us (5%)
  local copies, waits for them, and re-layouts  2.91 us (2%)
    ppermute x2, waiting for transfers between devices, from_behind(): return lax.ppermute(block, axis, route)  37.6 us
    ppermute x2, starting transfers between devices, from_behind(): return lax.ppermute(block, axis, route)  24 us
    all_to_all x2, blocking collectives, exchange(): return lax.all_to_all(blocks, 'fsdp', 0, 0, axis_index_groups=groups)  21.4 us
    ppermute x7, starting transfers between devices, swap(): return lax.ppermute(block, 'fsdp', [(i, i ^ k) for i in range(size)])  20 us
    ppermute x7, waiting for transfers between devices, swap(): return lax.ppermute(block, 'fsdp', [(i, i ^ k) for i in range(size)])  14.6 us
    all_to_all x1, starting transfers between devices, exchange(): return lax.all_to_all(blocks, 'fsdp', 0, 0, axis_index_groups=groups)  4.61 us
    all_to_all x1, waiting for transfers between devices, exchange(): return lax.all_to_all(blocks, 'fsdp', 0, 0, axis_index_groups=groups)  4.23 us
    unnamed x8, local copies, waits for them, and re-layouts  2.91 us
  transfers between devices with their start and end apart: 10, of which 7 were waited for; matrix products, arithmetic and copies ran while one was open for 0% of the time, Pallas kernels for 1%

profile of v5, /device:TPU:32, one launch (start us, length us, event | category | flops | bytes accessed | tf_op | source)
XLA Modules:
  0.0 137.0 jit_solution(17196367033017686170)
XLA Ops:
  0.0 2.6 %block.1 = bf16[4,4,128,512]{3,2,1,0:T(8,128)(2,1)} custom-call(bf16[128,8192]{1,0:T(8,128)(2,1)} %bitcast.8), custom_call_target="tpu_custom_call" | custom-call | tf_op jit(solution)/shard_map/block/pallas_call | solution.py:168
  2.7 4.6 %all-to-all-start = ((bf16[4,4,128,512]{3,2,1,0:T(8,128)(2,1)}), bf16[4,4,128,512]{3,2,1,0:T(8,128)(2,1)S(1)}, u32[]{:S(2)}, u32[]{:S(2)}) async-start(bf16[4,4,128,512]{3,2,1,0:T(8,128)(2,1)} %block.1), calls=%async_computation | async-start | bytes 4194304 | tf_op jit(solution)/shard_map/all_to_all | solution.py:150
  7.3 4.9 %collective-permute-start.1 = (bf16[512,512]{1,0:T(8,128)(2,1)S(1)}, bf16[512,512]{1,0:T(8,128)(2,1)S(1)}, u32[]{:S(2)}, u32[]{:S(2)}) collective-permute-start(bf16[512,512]{1,0:T(8,128)(2,1)S(1)} %round.1.refs_0_), channel_id=1, source_target_pairs={{0,2},{1,3},{2,0},{3,1},{4,6},{5,7},{6,4},{7,5},{8,10},{9,11},{10,... | collective-permute-start | bytes 1572872 | tf_op jit(solution)/shard_map/ppermute | solution.py:153
  12.3 1.9 %collective-permute-start = (bf16[512,512]{1,0:T(8,128)(2,1)S(1)}, bf16[512,512]{1,0:T(8,128)(2,1)S(1)}, u32[]{:S(2)}, u32[]{:S(2)}) collective-permute-start(bf16[512,512]{1,0:T(8,128)(2,1)S(1)} %round.1.refs_0_), channel_id=1, source_target_pairs={{0,1},{1,0},{2,3},{3,2},{4,5},{5,4},{6,7},{7,6},{8,9},{9,8},{10,11... | collective-permute-start | bytes 1572872 | tf_op jit(solution)/shard_map/ppermute | solution.py:153
  14.2 9.9 %collective-permute-done.1.refs_2_ = bf16[512,512]{1,0:T(8,128)(2,1)S(1)} collective-permute-done((bf16[512,512]{1,0:T(8,128)(2,1)S(1)}, bf16[512,512]{1,0:T(8,128)(2,1)S(1)}, u32[]{:S(2)}, u32[]{:S(2)}) %collective-permute-start.1) | collective-permute-done | bytes 524320 | tf_op jit(solution)/shard_map/ppermute | solution.py:153
  24.1 1.9 %collective-permute-start.2 = (bf16[512,512]{1,0:T(8,128)(2,1)S(1)}, bf16[512,512]{1,0:T(8,128)(2,1)S(1)}, u32[]{:S(2)}, u32[]{:S(2)}) collective-permute-start(bf16[512,512]{1,0:T(8,128)(2,1)S(1)} %collective-permute-done.1.refs_2_), channel_id=1, source_target_pairs={{0,1},{1,0},{2,3},{3,2},{4,5},{5,4},{6,7},{7,6},{8,9},{9,8},{10,11... | collective-permute-start | bytes 1572872 | tf_op jit(solution)/shard_map/ppermute | solution.py:153
  26.0 1.9 %collective-permute-done.2.refs_3_ = bf16[512,512]{1,0:T(8,128)(2,1)S(1)} collective-permute-done((bf16[512,512]{1,0:T(8,128)(2,1)S(1)}, bf16[512,512]{1,0:T(8,128)(2,1)S(1)}, u32[]{:S(2)}, u32[]{:S(2)}) %collective-permute-start.2) | collective-permute-done | bytes 524320 | tf_op jit(solution)/shard_map/ppermute | solution.py:153
  27.9 0.1 stack.1.working
  28.0 1.3 copy-done
  29.4 4.2 %all-to-all-done.blocks = bf16[4,4,128,512]{3,2,1,0:T(8,128)(2,1)S(1)} async-done(((bf16[4,4,128,512]{3,2,1,0:T(8,128)(2,1)}), bf16[4,4,128,512]{3,2,1,0:T(8,128)(2,1)S(1)}, u32[]{:S(2)}, u32[]{:S(2)}) %all-to-all-start) | async-done | bytes 2097184 | tf_op jit(solution)/shard_map/all_to_all | solution.py:150
  33.6 1.6 %copy-done.1 = bf16[4,512,512]{2,1,0:T(8,128)(2,1)S(1)} copy-done((bf16[4,512,512]{2,1,0:T(8,128)(2,1)S(1)}, bf16[4,512,512]{2,1,0:T(8,128)(2,1)}, u32[]{:S(2)}) %copy-start.1) | copy-done | bytes 2097176
  35.2 1.2 keys.1
  36.4 11.0 %all_to_all.15.parts = bf16[4,128,512]{2,1,0:T(8,128)(2,1)S(1)} all-to-all(bf16[4,128,512]{2,1,0:T(8,128)(2,1)S(1)} %keys.1), channel_id=1, replica_groups={{0,4,8,12},{1,5,9,13},{2,6,10,14},{3,7,11,15},{16,20,24,28},{17,21,25,2..., dimensions={0} | all-to-all | bytes 1048576 | tf_op jit(solution)/shard_map/all_to_all | solution.py:150
  47.4 0.1 error.1
  47.5 10.5 %all_to_all.16.errors = bf16[4,128,512]{2,1,0:T(8,128)(2,1)S(1)} all-to-all(bf16[4,128,512]{2,1,0:T(8,128)(2,1)S(1)} %error.1), channel_id=1, replica_groups={{0,4,8,12},{1,5,9,13},{2,6,10,14},{3,7,11,15},{16,20,24,28},{17,21,25,2..., dimensions={0} | all-to-all | bytes 1048576 | tf_op jit(solution)/shard_map/all_to_all | solution.py:150
  58.0 0.5 given_0.1._
  58.5 1.9 %collective-permute-start.3 = (bf16[2,512,256]{2,1,0:T(8,128)(2,1)S(1)}, bf16[2,512,256]{2,1,0:T(8,128)(2,1)S(1)}, u32[]{:S(2)}, u32[]{:S(2)}) collective-permute-start(bf16[2,512,256]{2,1,0:T(8,128)(2,1)S(1)} %given_0.1._), channel_id=1, source_target_pairs={{0,1},{1,0},{2,3},{3,2},{4,5},{5,4},{6,7},{7,6},{8,9},{9,8},{10,11... | collective-permute-start | bytes 1572872 | tf_op jit(solution)/shard_map/ppermute | solution.py:153
  60.4 0.5 kept_0.1
  60.9 1.4 %collective-permute-done.3.given = bf16[2,512,256]{2,1,0:T(8,128)(2,1)S(1)} collective-permute-done((bf16[2,512,256]{2,1,0:T(8,128)(2,1)S(1)}, bf16[2,512,256]{2,1,0:T(8,128)(2,1)S(1)}, u32[]{:S(2)}, u32[]{:S(2)}) %collective-permute-start.3) | collective-permute-done | bytes 524320 | tf_op jit(solution)/shard_map/ppermute | solution.py:153
  62.3 4.9 %collective-permute-start.4 = (bf16[512,256]{1,0:T(8,128)(2,1)S(1)}, bf16[512,256]{1,0:T(8,128)(2,1)S(1)}, u32[]{:S(2)}, u32[]{:S(2)}) collective-permute-start(bf16[512,256]{1,0:T(8,128)(2,1)S(1)} %across_0.1.rest_0_), channel_id=1, source_target_pairs={{0,2},{1,3},{2,0},{3,1},{4,6},{5,7},{6,4},{7,5},{8,10},{9,11},{10,... | collective-permute-start | bytes 786440 | tf_op jit(solution)/shard_map/ppermute | solution.py:153
  67.3 0.5 given_1.1._
  67.8 1.9 %collective-permute-start.6 = (bf16[2,512,256]{2,1,0:T(8,128)(2,1)S(1)}, bf16[2,512,256]{2,1,0:T(8,128)(2,1)S(1)}, u32[]{:S(2)}, u32[]{:S(2)}) collective-permute-start(bf16[2,512,256]{2,1,0:T(8,128)(2,1)S(1)} %given_1.1._), channel_id=1, source_target_pairs={{0,1},{1,0},{2,3},{3,2},{4,5},{5,4},{6,7},{7,6},{8,9},{9,8},{10,11... | collective-permute-start | bytes 1572872 | tf_op jit(solution)/shard_map/ppermute | solution.py:153
  69.7 0.5 kept_1.1
  70.2 1.4 %collective-permute-done.6.given = bf16[2,512,256]{2,1,0:T(8,128)(2,1)S(1)} collective-permute-done((bf16[2,512,256]{2,1,0:T(8,128)(2,1)S(1)}, bf16[2,512,256]{2,1,0:T(8,128)(2,1)S(1)}, u32[]{:S(2)}, u32[]{:S(2)}) %collective-permute-start.6) | collective-permute-done | bytes 524320 | tf_op jit(solution)/shard_map/ppermute | solution.py:153
  71.6 2.4 %collective-permute-start.7 = (bf16[512,256]{1,0:T(8,128)(2,1)S(1)}, bf16[512,256]{1,0:T(8,128)(2,1)S(1)}, u32[]{:S(2)}, u32[]{:S(2)}) collective-permute-start(bf16[512,256]{1,0:T(8,128)(2,1)S(1)} %across_1.1), channel_id=1, source_target_pairs={{0,2},{1,3},{2,0},{3,1},{4,6},{5,7},{6,4},{7,5},{8,10},{9,11},{10,... | collective-permute-start | bytes 786440 | tf_op jit(solution)/shard_map/ppermute | solution.py:153
  74.1 0.1 step_0.1
  74.2 14.8 %collective-permute-start.5 = (bf16[512,256]{1,0:T(8,128)(2,1)S(1)}, bf16[512,256]{1,0:T(8,128)(2,1)S(1)}, u32[]{:S(2)}, u32[]{:S(2)}) collective-permute-start(bf16[512,256]{1,0:T(8,128)(2,1)S(1)} %get-tuple-element.16), channel_id=1, source_target_pairs={{384,0},{400,16},{416,32},{432,48},{448,64},{464,80},{480,96},{496... | collective-permute-start | bytes 786440 | tf_op jit(solution)/shard_map/ppermute | solution.py:139
  89.0 0.1 step_1.1
  89.2 9.1 %collective-permute-start.8 = (bf16[512,256]{1,0:T(8,128)(2,1)S(1)}, bf16[512,256]{1,0:T(8,128)(2,1)S(1)}, u32[]{:S(2)}, u32[]{:S(2)}) collective-permute-start(bf16[512,256]{1,0:T(8,128)(2,1)S(1)} %get-tuple-element.20), channel_id=1, source_target_pairs={{384,0},{400,16},{416,32},{432,48},{448,64},{464,80},{480,96},{496... | collective-permute-start | bytes 786440 | tf_op jit(solution)/shard_map/ppermute | solution.py:139
  98.3 32.5 %collective-permute-done.5.other = bf16[512,256]{1,0:T(8,128)(2,1)S(1)} collective-permute-done((bf16[512,256]{1,0:T(8,128)(2,1)S(1)}, bf16[512,256]{1,0:T(8,128)(2,1)S(1)}, u32[]{:S(2)}, u32[]{:S(2)}) %collective-permute-start.5) | collective-permute-done | bytes 262176 | tf_op jit(solution)/shard_map/ppermute | solution.py:139
  130.9 5.0 %collective-permute-done.8.refs_2_ = bf16[512,256]{1,0:T(8,128)(2,1)S(1)} collective-permute-done((bf16[512,256]{1,0:T(8,128)(2,1)S(1)}, bf16[512,256]{1,0:T(8,128)(2,1)S(1)}, u32[]{:S(2)}, u32[]{:S(2)}) %collective-permute-start.8) | collective-permute-done | bytes 262176 | tf_op jit(solution)/shard_map/ppermute | solution.py:139
  135.9 1.1 average.1
  (13 shorter events, 0.3 us)
Async XLA Ops:
  2.6 4.6 %copy-start.2 = (f32[1,512,512]{2,1,0:T(8,128)S(1)}, f32[1,512,512]{2,1,0:T(8,128)}, u32[]{:S(2)}) copy-start(f32[1,512,512]{2,1,0:T(8,128)} %param.3) | copy-start | bytes 3145732
  2.7 30.9 %all-to-all-start = ((bf16[4,4,128,512]{3,2,1,0:T(8,128)(2,1)}), bf16[4,4,128,512]{3,2,1,0:T(8,128)(2,1)S(1)}, u32[]{:S(2)}, u32[]{:S(2)}) async-start(bf16[4,4,128,512]{3,2,1,0:T(8,128)(2,1)} %block.1), calls=%async_computation | async-start | bytes 4194304 | tf_op jit(solution)/shard_map/all_to_all | solution.py:150
  7.3 16.8 %collective-permute-start.1 = (bf16[512,512]{1,0:T(8,128)(2,1)S(1)}, bf16[512,512]{1,0:T(8,128)(2,1)S(1)}, u32[]{:S(2)}, u32[]{:S(2)}) collective-permute-start(bf16[512,512]{1,0:T(8,128)(2,1)S(1)} %round.1.refs_0_), channel_id=1, source_target_pairs={{0,2},{1,3},{2,0},{3,1},{4,6},{5,7},{6,4},{7,5},{8,10},{9,11},{10,... | collective-permute-start | bytes 1572872 | tf_op jit(solution)/shard_map/ppermute | solution.py:153
  12.3 13.8 %collective-permute-start = (bf16[512,512]{1,0:T(8,128)(2,1)S(1)}, bf16[512,512]{1,0:T(8,128)(2,1)S(1)}, u32[]{:S(2)}, u32[]{:S(2)}) collective-permute-start(bf16[512,512]{1,0:T(8,128)(2,1)S(1)} %round.1.refs_0_), channel_id=1, source_target_pairs={{0,1},{1,0},{2,3},{3,2},{4,5},{5,4},{6,7},{7,6},{8,9},{9,8},{10,11... | collective-permute-start | bytes 1572872 | tf_op jit(solution)/shard_map/ppermute | solution.py:153
  24.1 3.8 %collective-permute-start.2 = (bf16[512,512]{1,0:T(8,128)(2,1)S(1)}, bf16[512,512]{1,0:T(8,128)(2,1)S(1)}, u32[]{:S(2)}, u32[]{:S(2)}) collective-permute-start(bf16[512,512]{1,0:T(8,128)(2,1)S(1)} %collective-permute-done.1.refs_2_), channel_id=1, source_target_pairs={{0,1},{1,0},{2,3},{3,2},{4,5},{5,4},{6,7},{7,6},{8,9},{9,8},{10,11... | collective-permute-start | bytes 1572872 | tf_op jit(solution)/shard_map/ppermute | solution.py:153
  28.0 1.3 copy-start
  33.6 1.6 %copy-start.1 = (bf16[4,512,512]{2,1,0:T(8,128)(2,1)S(1)}, bf16[4,512,512]{2,1,0:T(8,128)(2,1)}, u32[]{:S(2)}) copy-start(bf16[4,512,512]{2,1,0:T(8,128)(2,1)} %copy-done) | copy-start | bytes 6291460
  35.2 12.2 %copy-start.3 = (bf16[1,128,512]{2,1,0:T(8,128)(2,1)S(1)}, bf16[1,128,512]{2,1,0:T(8,128)(2,1)}, u32[]{:S(2)}) copy-start(bf16[1,128,512]{2,1,0:T(8,128)(2,1)} %param.5) | copy-start | bytes 393220
  58.5 3.8 %collective-permute-start.3 = (bf16[2,512,256]{2,1,0:T(8,128)(2,1)S(1)}, bf16[2,512,256]{2,1,0:T(8,128)(2,1)S(1)}, u32[]{:S(2)}, u32[]{:S(2)}) collective-permute-start(bf16[2,512,256]{2,1,0:T(8,128)(2,1)S(1)} %given_0.1._), channel_id=1, source_target_pairs={{0,1},{1,0},{2,3},{3,2},{4,5},{5,4},{6,7},{7,6},{8,9},{9,8},{10,11... | collective-permute-start | bytes 1572872 | tf_op jit(solution)/shard_map/ppermute | solution.py:153
  62.3 11.7 %collective-permute-start.4 = (bf16[512,256]{1,0:T(8,128)(2,1)S(1)}, bf16[512,256]{1,0:T(8,128)(2,1)S(1)}, u32[]{:S(2)}, u32[]{:S(2)}) collective-permute-start(bf16[512,256]{1,0:T(8,128)(2,1)S(1)} %across_0.1.rest_0_), channel_id=1, source_target_pairs={{0,2},{1,3},{2,0},{3,1},{4,6},{5,7},{6,4},{7,5},{8,10},{9,11},{10,... | collective-permute-start | bytes 786440 | tf_op jit(solution)/shard_map/ppermute | solution.py:153
  67.8 3.8 %collective-permute-start.6 = (bf16[2,512,256]{2,1,0:T(8,128)(2,1)S(1)}, bf16[2,512,256]{2,1,0:T(8,128)(2,1)S(1)}, u32[]{:S(2)}, u32[]{:S(2)}) collective-permute-start(bf16[2,512,256]{2,1,0:T(8,128)(2,1)S(1)} %given_1.1._), channel_id=1, source_target_pairs={{0,1},{1,0},{2,3},{3,2},{4,5},{5,4},{6,7},{7,6},{8,9},{9,8},{10,11... | collective-permute-start | bytes 1572872 | tf_op jit(solution)/shard_map/ppermute | solution.py:153
  71.6 17.4 %collective-permute-start.7 = (bf16[512,256]{1,0:T(8,128)(2,1)S(1)}, bf16[512,256]{1,0:T(8,128)(2,1)S(1)}, u32[]{:S(2)}, u32[]{:S(2)}) collective-permute-start(bf16[512,256]{1,0:T(8,128)(2,1)S(1)} %across_1.1), channel_id=1, source_target_pairs={{0,2},{1,3},{2,0},{3,1},{4,6},{5,7},{6,4},{7,5},{8,10},{9,11},{10,... | collective-permute-start | bytes 786440 | tf_op jit(solution)/shard_map/ppermute | solution.py:153
  74.2 56.6 %collective-permute-start.5 = (bf16[512,256]{1,0:T(8,128)(2,1)S(1)}, bf16[512,256]{1,0:T(8,128)(2,1)S(1)}, u32[]{:S(2)}, u32[]{:S(2)}) collective-permute-start(bf16[512,256]{1,0:T(8,128)(2,1)S(1)} %get-tuple-element.16), channel_id=1, source_target_pairs={{384,0},{400,16},{416,32},{432,48},{448,64},{464,80},{480,96},{496... | collective-permute-start | bytes 786440 | tf_op jit(solution)/shard_map/ppermute | solution.py:139
  89.2 46.8 %collective-permute-start.8 = (bf16[512,256]{1,0:T(8,128)(2,1)S(1)}, bf16[512,256]{1,0:T(8,128)(2,1)S(1)}, u32[]{:S(2)}, u32[]{:S(2)}) collective-permute-start(bf16[512,256]{1,0:T(8,128)(2,1)S(1)} %get-tuple-element.20), channel_id=1, source_target_pairs={{384,0},{400,16},{416,32},{432,48},{448,64},{464,80},{480,96},{496... | collective-permute-start | bytes 786440 | tf_op jit(solution)/shard_map/ppermute | solution.py:139

commit v6 on v5

--- a/solution.py
+++ b/solution.py
@@ -40,17 +40,18 @@
 def block_kernel(features, blocks, held, sem):
     mine = lax.rem(lax.axis_index("fsdp"), SIDE)
     ring, _, _, rows = blocks.shape
-    places = [(y, k) for y in range(ring) for k in range(SIDE)]
     reads, writes = [], []
-    for y, k in places:
-        start = pl.multiple_of((y * SIDE + (mine ^ k)) * rows, rows)
-        source = features.at[:, pl.ds(start, rows)]
-        reads.append(pltpu.make_async_copy(source, held.at[y, k], sem.at[0, y, k]))
-        writes.append(pltpu.make_async_copy(held.at[y, k], blocks.at[y, k], sem.at[1, y, k]))
+    for y in range(ring):
+        source = features.at[:, pl.ds(y * SIDE * rows, SIDE * rows)]
+        reads.append(pltpu.make_async_copy(source, held.at[y], sem.at[0, y, 0]))
         reads[-1].start()
-    for read, write in zip(reads, writes):
-        read.wait()
-        write.start()
+    for y in range(ring):
+        reads[y].wait()
+        for k in range(SIDE):
+            start = pl.multiple_of((mine ^ k) * rows, rows)
+            source = held.at[y, :, pl.ds(start, rows)]
+            writes.append(pltpu.make_async_copy(source, blocks.at[y, k], sem.at[1, y, k]))
+            writes[-1].start()
     for write in writes:
         write.wait()
 
@@ -119,18 +120,12 @@
     sent[...] = new.astype(BF16)
 
 
-def mean_kernel(stepped, other, out):
-    out[...] = 0.5 * (stepped[...] + other[...].astype(F32))
-
-
-def average_kernel(*refs):
-    *means, stepped, other, out = refs
-    start = 0
-    for mean in means:
-        stop = start + mean.shape[1]
-        out[:, start:stop] = mean[...]
-        start = stop
-    out[:, start:] = 0.5 * (stepped[...] + other[...].astype(F32))
+def mean_kernel(start, stepped, other, *rest):
+    out, held, sem = rest[-3:]
+    held[...] = 0.5 * (stepped[...] + other[...].astype(F32))
+    copy = pltpu.make_async_copy(held, out.at[:, pl.ds(start, held.shape[1])], sem)
+    copy.start()
+    copy.wait()
 
 
 def from_behind(block, axis, distance):
@@ -171,7 +166,7 @@
         out_shape=jax.ShapeDtypeStruct(shape, BF16),
         in_specs=[pl.BlockSpec(memory_space=pl.ANY)],
         out_specs=pl.BlockSpec(memory_space=pl.ANY),
-        scratch_shapes=[pltpu.VMEM(shape, BF16), pltpu.SemaphoreType.DMA((2, ring, SIDE))],
+        scratch_shapes=[pltpu.VMEM((ring, count, SIDE * rows), BF16), pltpu.SemaphoreType.DMA((2, ring, SIDE))],
         compiler_params=pltpu.CompilerParams(vmem_limit_bytes=60 * 1024 * 1024),
     )(tokens)
     blocks = exchange(blocks)
@@ -211,13 +206,21 @@
             [VMEM] * 4,
             weight,
         )(kept, given, swap(across, 2), master)
-        result = (stepped, from_behind(sent, "rep", hop))
-        if h < len(chunks) - 1:
-            result = call(mean_kernel, f"mean_{h}", [(half, F32)], [VMEM] * 2, mean_weight)(*result)
-        results += result
-    (updated,) = call(average_kernel, "average", [((rows, width), F32)], [VMEM] * len(results))(
-        *results
-    )
+        results.append((start, half, mean_weight, stepped, from_behind(sent, "rep", hop)))
+    updated = []
+    for h, (start, half, weight, stepped, other) in enumerate(results):
+        updated = pl.pallas_call(
+            functools.partial(mean_kernel, start),
+            name=f"mean_{h}",
+            out_shape=[jax.ShapeDtypeStruct((rows, width), F32)],
+            in_specs=[VMEM] * 2 + [ANY] * len(updated),
+            out_specs=[ANY],
+            scratch_shapes=[pltpu.VMEM(half, F32), pltpu.SemaphoreType.DMA],
+            input_output_aliases={2: 0} if updated else {},
+            compiler_params=pltpu.CompilerParams(vmem_limit_bytes=8 * 1024 * 1024),
+            cost_estimate=pl.CostEstimate(flops=weight, bytes_accessed=1_000_000, transcendentals=0),
+        )(stepped, other, *updated)
+    (updated,) = updated
     return updated[None]
 
 

time: 138 us -> 137 us (level)
  transfers between devices with their start and end apart: 10 -> 10, of which waited for: 7 -> 7; matrix products, arithmetic and copies ran while one was open for 0% -> 0% of each run, Pallas kernels for 1% -> 2%
where the time goes in v6:
time: 137 us
  waiting for transfers between devices  55.5 us (41%)
  starting transfers between devices  48.5 us (35%)
  blocking collectives  21.4 us (16%)
  Pallas kernels  8.17 us (6%)
  local copies, waits for them, and re-layouts  2.91 us (2%)
    ppermute x2, waiting for transfers between devices, from_behind(): return lax.ppermute(block, axis, route)  36.7 us
    ppermute x2, starting transfers between devices, from_behind(): return lax.ppermute(block, axis, route)  24 us
    all_to_all x2, blocking collectives, exchange(): return lax.all_to_all(blocks, 'fsdp', 0, 0, axis_index_groups=groups)  21.4 us
    ppermute x7, starting transfers between devices, swap(): return lax.ppermute(block, 'fsdp', [(i, i ^ k) for i in range(size)])  19.9 us
    ppermute x7, waiting for transfers between devices, swap(): return lax.ppermute(block, 'fsdp', [(i, i ^ k) for i in range(size)])  14.6 us
    all_to_all x1, starting transfers between devices, exchange(): return lax.all_to_all(blocks, 'fsdp', 0, 0, axis_index_groups=groups)  4.61 us
    all_to_all x1, waiting for transfers between devices, exchange(): return lax.all_to_all(blocks, 'fsdp', 0, 0, axis_index_groups=groups)  4.23 us
    unnamed x8, local copies, waits for them, and re-layouts  2.91 us
  transfers between devices with their start and end apart: 10, of which 7 were waited for; matrix products, arithmetic and copies ran while one was open for 0% of the time, Pallas kernels for 2%

profile of v6, /device:TPU:32, one launch (start us, length us, event | category | flops | bytes accessed | tf_op | source)
XLA Modules:
  0.0 136.8 jit_solution(871003577981044817)
XLA Ops:
  0.0 2.7 %block.1 = bf16[4,4,128,512]{3,2,1,0:T(8,128)(2,1)} custom-call(bf16[128,8192]{1,0:T(8,128)(2,1)} %bitcast.8), custom_call_target="tpu_custom_call" | custom-call | tf_op jit(solution)/shard_map/block/pallas_call | solution.py:163
  2.7 4.6 %all-to-all-start = ((bf16[4,4,128,512]{3,2,1,0:T(8,128)(2,1)}), bf16[4,4,128,512]{3,2,1,0:T(8,128)(2,1)S(1)}, u32[]{:S(2)}, u32[]{:S(2)}) async-start(bf16[4,4,128,512]{3,2,1,0:T(8,128)(2,1)} %block.1), calls=%async_computation | async-start | bytes 4194304 | tf_op jit(solution)/shard_map/all_to_all | solution.py:145
  7.4 4.9 %collective-permute-start.1 = (bf16[512,512]{1,0:T(8,128)(2,1)S(1)}, bf16[512,512]{1,0:T(8,128)(2,1)S(1)}, u32[]{:S(2)}, u32[]{:S(2)}) collective-permute-start(bf16[512,512]{1,0:T(8,128)(2,1)S(1)} %round.1.refs_0_), channel_id=1, source_target_pairs={{0,2},{1,3},{2,0},{3,1},{4,6},{5,7},{6,4},{7,5},{8,10},{9,11},{10,... | collective-permute-start | bytes 1572872 | tf_op jit(solution)/shard_map/ppermute | solution.py:148
  12.3 1.9 %collective-permute-start = (bf16[512,512]{1,0:T(8,128)(2,1)S(1)}, bf16[512,512]{1,0:T(8,128)(2,1)S(1)}, u32[]{:S(2)}, u32[]{:S(2)}) collective-permute-start(bf16[512,512]{1,0:T(8,128)(2,1)S(1)} %round.1.refs_0_), channel_id=1, source_target_pairs={{0,1},{1,0},{2,3},{3,2},{4,5},{5,4},{6,7},{7,6},{8,9},{9,8},{10,11... | collective-permute-start | bytes 1572872 | tf_op jit(solution)/shard_map/ppermute | solution.py:148
  14.2 9.9 %collective-permute-done.1.refs_2_ = bf16[512,512]{1,0:T(8,128)(2,1)S(1)} collective-permute-done((bf16[512,512]{1,0:T(8,128)(2,1)S(1)}, bf16[512,512]{1,0:T(8,128)(2,1)S(1)}, u32[]{:S(2)}, u32[]{:S(2)}) %collective-permute-start.1) | collective-permute-done | bytes 524320 | tf_op jit(solution)/shard_map/ppermute | solution.py:148
  24.1 1.9 %collective-permute-start.2 = (bf16[512,512]{1,0:T(8,128)(2,1)S(1)}, bf16[512,512]{1,0:T(8,128)(2,1)S(1)}, u32[]{:S(2)}, u32[]{:S(2)}) collective-permute-start(bf16[512,512]{1,0:T(8,128)(2,1)S(1)} %collective-permute-done.1.refs_2_), channel_id=1, source_target_pairs={{0,1},{1,0},{2,3},{3,2},{4,5},{5,4},{6,7},{7,6},{8,9},{9,8},{10,11... | collective-permute-start | bytes 1572872 | tf_op jit(solution)/shard_map/ppermute | solution.py:148
  26.1 1.9 %collective-permute-done.2.refs_3_ = bf16[512,512]{1,0:T(8,128)(2,1)S(1)} collective-permute-done((bf16[512,512]{1,0:T(8,128)(2,1)S(1)}, bf16[512,512]{1,0:T(8,128)(2,1)S(1)}, u32[]{:S(2)}, u32[]{:S(2)}) %collective-permute-start.2) | collective-permute-done | bytes 524320 | tf_op jit(solution)/shard_map/ppermute | solution.py:148
  27.9 0.1 stack.1.working
  28.1 1.3 copy-done
  29.4 4.2 %all-to-all-done.blocks = bf16[4,4,128,512]{3,2,1,0:T(8,128)(2,1)S(1)} async-done(((bf16[4,4,128,512]{3,2,1,0:T(8,128)(2,1)}), bf16[4,4,128,512]{3,2,1,0:T(8,128)(2,1)S(1)}, u32[]{:S(2)}, u32[]{:S(2)}) %all-to-all-start) | async-done | bytes 2097184 | tf_op jit(solution)/shard_map/all_to_all | solution.py:145
  33.6 1.6 %copy-done.1 = bf16[4,512,512]{2,1,0:T(8,128)(2,1)S(1)} copy-done((bf16[4,512,512]{2,1,0:T(8,128)(2,1)S(1)}, bf16[4,512,512]{2,1,0:T(8,128)(2,1)}, u32[]{:S(2)}) %copy-start.1) | copy-done | bytes 2097176
  35.2 1.2 keys.1
  36.5 11.0 %all_to_all.15.parts = bf16[4,128,512]{2,1,0:T(8,128)(2,1)S(1)} all-to-all(bf16[4,128,512]{2,1,0:T(8,128)(2,1)S(1)} %keys.1), channel_id=1, replica_groups={{0,4,8,12},{1,5,9,13},{2,6,10,14},{3,7,11,15},{16,20,24,28},{17,21,25,2..., dimensions={0} | all-to-all | bytes 1048576 | tf_op jit(solution)/shard_map/all_to_all | solution.py:145
  47.5 10.5 %all_to_all.16.errors = bf16[4,128,512]{2,1,0:T(8,128)(2,1)S(1)} all-to-all(bf16[4,128,512]{2,1,0:T(8,128)(2,1)S(1)} %error.1), channel_id=1, replica_groups={{0,4,8,12},{1,5,9,13},{2,6,10,14},{3,7,11,15},{16,20,24,28},{17,21,25,2..., dimensions={0} | all-to-all | bytes 1048576 | tf_op jit(solution)/shard_map/all_to_all | solution.py:145
  58.0 0.5 given_0.1._
  58.5 1.9 %collective-permute-start.3 = (bf16[2,512,256]{2,1,0:T(8,128)(2,1)S(1)}, bf16[2,512,256]{2,1,0:T(8,128)(2,1)S(1)}, u32[]{:S(2)}, u32[]{:S(2)}) collective-permute-start(bf16[2,512,256]{2,1,0:T(8,128)(2,1)S(1)} %given_0.1._), channel_id=1, source_target_pairs={{0,1},{1,0},{2,3},{3,2},{4,5},{5,4},{6,7},{7,6},{8,9},{9,8},{10,11... | collective-permute-start | bytes 1572872 | tf_op jit(solution)/shard_map/ppermute | solution.py:148
  60.4 0.5 kept_0.1
  60.9 1.4 %collective-permute-done.3.given = bf16[2,512,256]{2,1,0:T(8,128)(2,1)S(1)} collective-permute-done((bf16[2,512,256]{2,1,0:T(8,128)(2,1)S(1)}, bf16[2,512,256]{2,1,0:T(8,128)(2,1)S(1)}, u32[]{:S(2)}, u32[]{:S(2)}) %collective-permute-start.3) | collective-permute-done | bytes 524320 | tf_op jit(solution)/shard_map/ppermute | solution.py:148
  62.4 4.9 %collective-permute-start.7 = (bf16[512,256]{1,0:T(8,128)(2,1)S(1)}, bf16[512,256]{1,0:T(8,128)(2,1)S(1)}, u32[]{:S(2)}, u32[]{:S(2)}) collective-permute-start(bf16[512,256]{1,0:T(8,128)(2,1)S(1)} %across_0.1.rest_0_), channel_id=1, source_target_pairs={{0,2},{1,3},{2,0},{3,1},{4,6},{5,7},{6,4},{7,5},{8,10},{9,11},{10,... | collective-permute-start | bytes 786440 | tf_op jit(solution)/shard_map/ppermute | solution.py:148
  67.3 0.5 given_1.1._
  67.8 1.9 %collective-permute-start.4 = (bf16[2,512,256]{2,1,0:T(8,128)(2,1)S(1)}, bf16[2,512,256]{2,1,0:T(8,128)(2,1)S(1)}, u32[]{:S(2)}, u32[]{:S(2)}) collective-permute-start(bf16[2,512,256]{2,1,0:T(8,128)(2,1)S(1)} %given_1.1._), channel_id=1, source_target_pairs={{0,1},{1,0},{2,3},{3,2},{4,5},{5,4},{6,7},{7,6},{8,9},{9,8},{10,11... | collective-permute-start | bytes 1572872 | tf_op jit(solution)/shard_map/ppermute | solution.py:148
  69.7 0.5 kept_1.1
  70.2 1.4 %collective-permute-done.4.given = bf16[2,512,256]{2,1,0:T(8,128)(2,1)S(1)} collective-permute-done((bf16[2,512,256]{2,1,0:T(8,128)(2,1)S(1)}, bf16[2,512,256]{2,1,0:T(8,128)(2,1)S(1)}, u32[]{:S(2)}, u32[]{:S(2)}) %collective-permute-start.4) | collective-permute-done | bytes 524320 | tf_op jit(solution)/shard_map/ppermute | solution.py:148
  71.7 2.4 %collective-permute-start.5 = (bf16[512,256]{1,0:T(8,128)(2,1)S(1)}, bf16[512,256]{1,0:T(8,128)(2,1)S(1)}, u32[]{:S(2)}, u32[]{:S(2)}) collective-permute-start(bf16[512,256]{1,0:T(8,128)(2,1)S(1)} %across_1.1), channel_id=1, source_target_pairs={{0,2},{1,3},{2,0},{3,1},{4,6},{5,7},{6,4},{7,5},{8,10},{9,11},{10,... | collective-permute-start | bytes 786440 | tf_op jit(solution)/shard_map/ppermute | solution.py:148
  74.1 0.1 step_0.1
  74.2 14.8 %collective-permute-start.8 = (bf16[512,256]{1,0:T(8,128)(2,1)S(1)}, bf16[512,256]{1,0:T(8,128)(2,1)S(1)}, u32[]{:S(2)}, u32[]{:S(2)}) collective-permute-start(bf16[512,256]{1,0:T(8,128)(2,1)S(1)} %get-tuple-element.20), channel_id=1, source_target_pairs={{384,0},{400,16},{416,32},{432,48},{448,64},{464,80},{480,96},{496... | collective-permute-start | bytes 786440 | tf_op jit(solution)/shard_map/ppermute | solution.py:134
  89.1 0.1 step_1.1
  89.2 9.1 %collective-permute-start.6 = (bf16[512,256]{1,0:T(8,128)(2,1)S(1)}, bf16[512,256]{1,0:T(8,128)(2,1)S(1)}, u32[]{:S(2)}, u32[]{:S(2)}) collective-permute-start(bf16[512,256]{1,0:T(8,128)(2,1)S(1)} %get-tuple-element.17), channel_id=1, source_target_pairs={{384,0},{400,16},{416,32},{432,48},{448,64},{464,80},{480,96},{496... | collective-permute-start | bytes 786440 | tf_op jit(solution)/shard_map/ppermute | solution.py:134
  98.4 32.8 %collective-permute-done.8.other = bf16[512,256]{1,0:T(8,128)(2,1)S(1)} collective-permute-done((bf16[512,256]{1,0:T(8,128)(2,1)S(1)}, bf16[512,256]{1,0:T(8,128)(2,1)S(1)}, u32[]{:S(2)}, u32[]{:S(2)}) %collective-permute-start.8) | collective-permute-done | bytes 262176 | tf_op jit(solution)/shard_map/ppermute | solution.py:134
  131.1 0.9 mean_0.1.rest_0_
  132.0 3.9 %collective-permute-done.6.other = bf16[512,256]{1,0:T(8,128)(2,1)S(1)} collective-permute-done((bf16[512,256]{1,0:T(8,128)(2,1)S(1)}, bf16[512,256]{1,0:T(8,128)(2,1)S(1)}, u32[]{:S(2)}, u32[]{:S(2)}) %collective-permute-start.6) | collective-permute-done | bytes 262176 | tf_op jit(solution)/shard_map/ppermute | solution.py:134
  135.9 0.9 mean_1.1
  (13 shorter events, 0.3 us)
Async XLA Ops:
  2.7 4.6 %copy-start.2 = (f32[1,512,512]{2,1,0:T(8,128)S(1)}, f32[1,512,512]{2,1,0:T(8,128)}, u32[]{:S(2)}) copy-start(f32[1,512,512]{2,1,0:T(8,128)} %param.3) | copy-start | bytes 3145732
  2.7 30.9 %all-to-all-start = ((bf16[4,4,128,512]{3,2,1,0:T(8,128)(2,1)}), bf16[4,4,128,512]{3,2,1,0:T(8,128)(2,1)S(1)}, u32[]{:S(2)}, u32[]{:S(2)}) async-start(bf16[4,4,128,512]{3,2,1,0:T(8,128)(2,1)} %block.1), calls=%async_computation | async-start | bytes 4194304 | tf_op jit(solution)/shard_map/all_to_all | solution.py:145
  7.4 16.8 %collective-permute-start.1 = (bf16[512,512]{1,0:T(8,128)(2,1)S(1)}, bf16[512,512]{1,0:T(8,128)(2,1)S(1)}, u32[]{:S(2)}, u32[]{:S(2)}) collective-permute-start(bf16[512,512]{1,0:T(8,128)(2,1)S(1)} %round.1.refs_0_), channel_id=1, source_target_pairs={{0,2},{1,3},{2,0},{3,1},{4,6},{5,7},{6,4},{7,5},{8,10},{9,11},{10,... | collective-permute-start | bytes 1572872 | tf_op jit(solution)/shard_map/ppermute | solution.py:148
  12.3 13.8 %collective-permute-start = (bf16[512,512]{1,0:T(8,128)(2,1)S(1)}, bf16[512,512]{1,0:T(8,128)(2,1)S(1)}, u32[]{:S(2)}, u32[]{:S(2)}) collective-permute-start(bf16[512,512]{1,0:T(8,128)(2,1)S(1)} %round.1.refs_0_), channel_id=1, source_target_pairs={{0,1},{1,0},{2,3},{3,2},{4,5},{5,4},{6,7},{7,6},{8,9},{9,8},{10,11... | collective-permute-start | bytes 1572872 | tf_op jit(solution)/shard_map/ppermute | solution.py:148
  24.1 3.8 %collective-permute-start.2 = (bf16[512,512]{1,0:T(8,128)(2,1)S(1)}, bf16[512,512]{1,0:T(8,128)(2,1)S(1)}, u32[]{:S(2)}, u32[]{:S(2)}) collective-permute-start(bf16[512,512]{1,0:T(8,128)(2,1)S(1)} %collective-permute-done.1.refs_2_), channel_id=1, source_target_pairs={{0,1},{1,0},{2,3},{3,2},{4,5},{5,4},{6,7},{7,6},{8,9},{9,8},{10,11... | collective-permute-start | bytes 1572872 | tf_op jit(solution)/shard_map/ppermute | solution.py:148
  28.1 1.3 copy-start
  33.6 1.6 %copy-start.1 = (bf16[4,512,512]{2,1,0:T(8,128)(2,1)S(1)}, bf16[4,512,512]{2,1,0:T(8,128)(2,1)}, u32[]{:S(2)}) copy-start(bf16[4,512,512]{2,1,0:T(8,128)(2,1)} %copy-done) | copy-start | bytes 6291460
  35.2 12.2 %copy-start.3 = (bf16[1,128,512]{2,1,0:T(8,128)(2,1)S(1)}, bf16[1,128,512]{2,1,0:T(8,128)(2,1)}, u32[]{:S(2)}) copy-start(bf16[1,128,512]{2,1,0:T(8,128)(2,1)} %param.5) | copy-start | bytes 393220
  58.5 3.8 %collective-permute-start.3 = (bf16[2,512,256]{2,1,0:T(8,128)(2,1)S(1)}, bf16[2,512,256]{2,1,0:T(8,128)(2,1)S(1)}, u32[]{:S(2)}, u32[]{:S(2)}) collective-permute-start(bf16[2,512,256]{2,1,0:T(8,128)(2,1)S(1)} %given_0.1._), channel_id=1, source_target_pairs={{0,1},{1,0},{2,3},{3,2},{4,5},{5,4},{6,7},{7,6},{8,9},{9,8},{10,11... | collective-permute-start | bytes 1572872 | tf_op jit(solution)/shard_map/ppermute | solution.py:148
  62.4 11.7 %collective-permute-start.7 = (bf16[512,256]{1,0:T(8,128)(2,1)S(1)}, bf16[512,256]{1,0:T(8,128)(2,1)S(1)}, u32[]{:S(2)}, u32[]{:S(2)}) collective-permute-start(bf16[512,256]{1,0:T(8,128)(2,1)S(1)} %across_0.1.rest_0_), channel_id=1, source_target_pairs={{0,2},{1,3},{2,0},{3,1},{4,6},{5,7},{6,4},{7,5},{8,10},{9,11},{10,... | collective-permute-start | bytes 786440 | tf_op jit(solution)/shard_map/ppermute | solution.py:148
  67.8 3.8 %collective-permute-start.4 = (bf16[2,512,256]{2,1,0:T(8,128)(2,1)S(1)}, bf16[2,512,256]{2,1,0:T(8,128)(2,1)S(1)}, u32[]{:S(2)}, u32[]{:S(2)}) collective-permute-start(bf16[2,512,256]{2,1,0:T(8,128)(2,1)S(1)} %given_1.1._), channel_id=1, source_target_pairs={{0,1},{1,0},{2,3},{3,2},{4,5},{5,4},{6,7},{7,6},{8,9},{9,8},{10,11... | collective-permute-start | bytes 1572872 | tf_op jit(solution)/shard_map/ppermute | solution.py:148
  71.7 17.4 %collective-permute-start.5 = (bf16[512,256]{1,0:T(8,128)(2,1)S(1)}, bf16[512,256]{1,0:T(8,128)(2,1)S(1)}, u32[]{:S(2)}, u32[]{:S(2)}) collective-permute-start(bf16[512,256]{1,0:T(8,128)(2,1)S(1)} %across_1.1), channel_id=1, source_target_pairs={{0,2},{1,3},{2,0},{3,1},{4,6},{5,7},{6,4},{7,5},{8,10},{9,11},{10,... | collective-permute-start | bytes 786440 | tf_op jit(solution)/shard_map/ppermute | solution.py:148
  74.2 56.9 %collective-permute-start.8 = (bf16[512,256]{1,0:T(8,128)(2,1)S(1)}, bf16[512,256]{1,0:T(8,128)(2,1)S(1)}, u32[]{:S(2)}, u32[]{:S(2)}) collective-permute-start(bf16[512,256]{1,0:T(8,128)(2,1)S(1)} %get-tuple-element.20), channel_id=1, source_target_pairs={{384,0},{400,16},{416,32},{432,48},{448,64},{464,80},{480,96},{496... | collective-permute-start | bytes 786440 | tf_op jit(solution)/shard_map/ppermute | solution.py:134
  89.2 46.7 %collective-permute-start.6 = (bf16[512,256]{1,0:T(8,128)(2,1)S(1)}, bf16[512,256]{1,0:T(8,128)(2,1)S(1)}, u32[]{:S(2)}, u32[]{:S(2)}) collective-permute-start(bf16[512,256]{1,0:T(8,128)(2,1)S(1)} %get-tuple-element.17), channel_id=1, source_target_pairs={{384,0},{400,16},{416,32},{432,48},{448,64},{464,80},{480,96},{496... | collective-permute-start | bytes 786440 | tf_op jit(solution)/shard_map/ppermute | solution.py:134
